TPU v7x, 512 devices: a whole 4x4x16 slice. The times are simulated.
512 devices in a mesh: dp: 16 (over z), mp: 32 (over x, y, core).
Axes of the slice: x: 4, y: 4, z: 16, core: 2. Of those that a mesh axis runs over, the one named last changes fastest.
Arguments:
- activations: bfloat16 [8192, 8192], P('dp', 'mp'), may hold values from -6 to 6
- out_grads: bfloat16 [8192, 29568], P('dp', 'mp'), may hold values from -0.5 to 0.5
- test_matrix: bfloat16 [29568, 512], P('mp'), may hold values from -0.03125 to 0.03125
- first_moment: float32 [512, 29568], P('dp', 'mp'), may hold values from -12 to 12
- second_moment: float32 [512, 29568], P('dp', 'mp'), may hold values from 0.01 to 0.1
Outputs:
- update: bfloat16 [32, 256, 29568], P(None, 'dp', 'mp')
- new_first: float32 [512, 29568], P('dp', 'mp')
- new_second: float32 [512, 29568], P('dp', 'mp')
All inputs are finite; a program needn't handle non-finite values.
Results may differ from a plain program's by a relative error of at most 0.013.
Values may be sent and summed in bfloat16 or wider, within the bound.
A program may use at most 64 MiB of HBM per device.

v0:
```python
import jax
import jax.numpy as jnp
from jax import lax
from jax.sharding import PartitionSpec as P

FF = 29568
R = 512
STEP = 100


beta_one = 0.9
beta_two = 0.999
adam_eps = 1e-08
norm_eps = 1e-06


def orthonormal(rows_block, gram_matrix):
    lower_factor = jnp.linalg.cholesky(gram_matrix)
    return lax.linalg.triangular_solve(
        lower_factor, rows_block, left_side=False, lower=True, transpose_a=True
    )


def shards(activations, out_grads, test_matrix, first_moment, second_moment):
    width_local = activations.shape[1]
    dp_size = lax.axis_size("dp")
    slot_count = width_local // dp_size
    partial_in = jnp.dot(out_grads, test_matrix, preferred_element_type=jnp.float32)
    sketch_in = lax.psum(partial_in, "mp").astype(jnp.bfloat16)
    local_sketch = jnp.einsum(
        "td,tr->dr", activations, sketch_in, preferred_element_type=jnp.float32
    )
    sketch = lax.psum(local_sketch, "dp")
    gram_local = jnp.dot(
        sketch.T, sketch, precision=lax.Precision.HIGHEST, preferred_element_type=jnp.float32
    )
    gram_matrix = lax.psum(gram_local, "mp")
    basis_b = orthonormal(sketch, gram_matrix).astype(jnp.bfloat16)
    own_rows = lax.dynamic_slice_in_dim(basis_b, lax.axis_index("dp") * slot_count, slot_count, 0)
    partial_coords = jnp.dot(activations, basis_b, preferred_element_type=jnp.float32)
    coords = lax.psum(partial_coords, "mp").astype(jnp.bfloat16)
    columns = coords
    projected = lax.psum_scatter(
        jnp.einsum("tr,tf->rf", columns, out_grads, preferred_element_type=jnp.float32),
        "dp",
        scatter_dimension=0,
        tiled=True,
    )
    new_first = beta_one * first_moment + (1.0 - beta_one) * projected
    new_second = beta_two * second_moment + (1.0 - beta_two) * projected * projected
    correct_one = 1.0 - beta_one**STEP
    correct_two = 1.0 - beta_two**STEP
    direction = new_first / correct_one / (jnp.sqrt(new_second / correct_two) + adam_eps)
    squares = jnp.sum(direction * direction)
    total_squares = lax.psum(squares, ("dp", "mp"))
    entry_count = R * FF
    factor = lax.rsqrt(total_squares / entry_count + norm_eps)
    direction_b = direction.astype(jnp.bfloat16)
    slot_basis = lax.all_gather(own_rows, "mp", axis=0, tiled=True)
    columns = slot_basis
    product = jnp.dot(
        columns,
        lax.all_gather(direction_b, "dp", axis=0, tiled=True),
        preferred_element_type=jnp.float32,
    )
    block_count = lax.axis_size("mp")
    update = (
        (factor * product).astype(jnp.bfloat16).reshape(block_count, slot_count, out_grads.shape[1])
    )
    return (update, new_first, new_second)


def solution(mesh):
    placed = (P("dp", "mp"), P("dp", "mp"), P("mp", None), P("dp", "mp"), P("dp", "mp"))
    return jax.shard_map(
        shards,
        mesh=mesh,
        in_specs=placed,
        out_specs=(P(None, "dp", "mp"), P("dp", "mp"), P("dp", "mp")),
        check_vma=False,
    )
```

profile of v0, /device:TPU:1, one launch (start us, length us, event | category | flops | bytes accessed | tf_op | source)
XLA Modules:
  0.0 930.0 jit_solution(2423457155301430978)
XLA Ops:
  8.4 1.9 fusion.39
  10.3 135.2 %all-reduce.9 = bf16[512,512]{1,0:T(8,128)(2,1)S(1)} all-reduce(f32[512,512]{1,0:T(8,128)S(1)} %fusion.39), channel_id=1, replica_groups=mesh['dp'=16,'mp'=32] {'mp'}, use_global_device_ids=true, to_apply=%region_0.0 | all-reduce | flops 262144 | bytes 1572864 | tf_op jit(solution)/shard_map/psum | solution.py:29
  146.7 131.1 %all-reduce.6.cloned.1.call-done = f32[256,512]{0,1:T(8,128)} async-done(((f32[256,512]{0,1:T(8,128)}), f32[256,512]{0,1:T(8,128)}) %all-reduce.6.cloned.1.call-update) | async-done | bytes 524304 | tf_op jit(solution)/shard_map/psum | solution.py:33
  277.9 3.2 fusion.40
  281.4 142.4 %all-reduce.8.cloned.1.call-done = f32[512,512]{0,1:T(8,128)} async-done(((f32[512,512]{0,1:T(8,128)}), f32[512,512]{0,1:T(8,128)}) %all-reduce.8.cloned.1.call-update) | async-done | bytes 1048592 | tf_op jit(solution)/shard_map/psum | solution.py:37
  426.6 11.7 %cholesky.104 = f32[128,128]{1,0:T(8,128)S(1)} custom-call(f32[128,128]{1,0:T(8,128)S(1)} %cholesky.266), custom_call_target="Cholesky" | custom-call | tf_op jit(solution)/shard_map/jit(cholesky)/cholesky | solution.py:18
  438.4 9.8 %custom-call.30 = f32[1,128,128]{1,2,0:T(8,128)S(1)} custom-call(f32[1,128,128]{2,1,0:T(8,128)S(1)} %get-tuple-element.36), custom_call_target="InvertDiagBlocksLowerTriangular" | custom-call | tf_op jit(solution)/shard_map/jit(cholesky)/cholesky | solution.py:18
  450.9 11.7 %cholesky.217 = f32[128,128]{1,0:T(8,128)S(1)} custom-call(f32[128,128]{1,0:T(8,128)S(1)} %cholesky.270), custom_call_target="Cholesky" | custom-call | tf_op jit(solution)/shard_map/jit(cholesky)/cholesky | solution.py:18
  462.6 10.0 %custom-call.31 = f32[1,128,128]{1,2,0:T(8,128)S(1)} custom-call(f32[1,128,128]{2,1,0:T(8,128)S(1)} %get-tuple-element.33), custom_call_target="InvertDiagBlocksLowerTriangular" | custom-call | tf_op jit(solution)/shard_map/jit(cholesky)/cholesky | solution.py:18
  474.2 11.7 %cholesky.238 = f32[128,128]{1,0:T(8,128)S(1)} custom-call(f32[128,128]{1,0:T(8,128)S(1)} %cholesky.275), custom_call_target="Cholesky" | custom-call | tf_op jit(solution)/shard_map/jit(cholesky)/cholesky | solution.py:18
  486.7 9.8 %custom-call.32 = f32[1,128,128]{1,2,0:T(8,128)S(1)} custom-call(f32[1,128,128]{2,1,0:T(8,128)S(1)} %get-tuple-element.30), custom_call_target="InvertDiagBlocksLowerTriangular" | custom-call | tf_op jit(solution)/shard_map/jit(cholesky)/cholesky | solution.py:18
  497.9 11.7 %cholesky.255 = f32[128,128]{1,0:T(8,128)S(1)} custom-call(f32[128,128]{1,0:T(8,128)S(1)} %convolution_subtract_fusion.5), custom_call_target="Cholesky" | custom-call | tf_op jit(solution)/shard_map/jit(cholesky)/cholesky | solution.py:18
  514.8 14.4 %while.1 = (s32[]{:T(128)}, f32[512,512]{1,0:T(8,128)}, s32[4,2]{0,1:T(2,128)S(1)}, f32[4,128,128]{2,1,0:T(8,128)}, s32[]{:T(128)}) while((s32[]{:T(128)}, f32[512,512]{1,0:T(8,128)}, s32[4,2]{0,1:T(2,128)S(1)}, f32[4,128,128]{2,1,0:T(8,128)}, s32[]{:T(128)}) %tuple.37), condition=%wide.while_cond, body=%wide.while_body.sunk | while | flops 2 | bytes 132705 | solution.py:19
  515.5 3.0 bitcast_dynamic-update-slice_fusion.2
  519.1 3.0 bitcast_dynamic-update-slice_fusion.2
  522.8 3.0 bitcast_dynamic-update-slice_fusion.2
  526.4 2.9 bitcast_dynamic-update-slice_fusion.2
  529.3 40.1 %custom-call.33 = f32[4,128,128]{1,2,0:T(8,128)S(1)} custom-call(f32[4,128,128]{2,1,0:T(8,128)} %get-tuple-element.10), custom_call_target="InvertDiagBlocksLowerTriangular" | custom-call | tf_op jit(solution)/shard_map/triangular_solve | solution.py:19
  574.7 132.5 %all-reduce.10 = bf16[512,512]{0,1:T(8,128)(2,1)S(1)} all-reduce(f32[512,512]{0,1:T(8,128)S(1)} %convolution_bitcast_fusion), channel_id=1, replica_groups=mesh['dp'=16,'mp'=32] {'mp'}, use_global_device_ids=true, to_apply=%region_11.12 | all-reduce | flops 262144 | bytes 1572864 | tf_op jit(solution)/shard_map/psum | solution.py:41
  707.2 2.1 fusion.41
  709.6 27.4 %all_gather.6 = bf16[512,512]{1,0:T(8,128)(2,1)S(1)} all-gather(bf16[16,512]{1,0:T(8,128)(2,1)S(1)} %copy.19), channel_id=1, replica_groups=mesh['dp'=16,'mp'=32] {'mp'}, dimensions={0}, use_global_device_ids=true | all-gather | bytes 540672 | tf_op jit(solution)/shard_map/all_gather | solution.py:59
  737.0 37.0 %reduce-scatter.2.cloned.1.call-done = f32[32,924]{1,0:T(8,128)} async-done(((f32[512,924]{1,0:T(8,128)}), f32[32,924]{1,0:T(8,128)}) %reduce-scatter.2.cloned.1.call-update) | async-done | bytes 118288 | tf_op jit(solution)/shard_map/reduce_scatter | solution.py:43
  776.4 27.5 %all_gather.7 = bf16[512,924]{1,0:T(8,128)(2,1)S(1)} all-gather(bf16[32,924]{1,0:T(8,128)(2,1)S(1)} %fusion.33), channel_id=1, replica_groups=mesh['dp'=16,'mp'=32] {'dp'}, dimensions={0}, use_global_device_ids=true | all-gather | bytes 1005312 | tf_op jit(solution)/shard_map/all_gather | solution.py:63
  803.8 116.9 %psum.39 = f32[]{:T(128)} all-reduce(f32[]{:T(128)} %get-tuple-element.22), channel_id=1, replica_groups=mesh['dp'=16,'mp'=32] {'dp','mp'}, use_global_device_ids=true, to_apply=%region_14.15 | all-reduce | flops 1 | bytes 8 | tf_op jit(solution)/shard_map/psum | solution.py:55
  (71 shorter events, 27.1 us)
Async XLA Ops:
  7.2 1.2 copy-start
  7.2 138.3 %copy-start.4 = (bf16[512,256]{1,0:T(8,128)(2,1)S(1)}, bf16[512,256]{1,0:T(8,128)(2,1)}, u32[]{:S(2)}) copy-start(bf16[512,256]{1,0:T(8,128)(2,1)} %param.5) | copy-start | bytes 786436
  7.2 270.7 %all-reduce.6.cloned.1.call-start = ((), (), s32[]{:S(2)}) async-start(), calls=%async_computation.1 | async-start | bytes 1048576 | tf_op jit(solution)/shard_map/psum | solution.py:33
  146.7 277.1 %all-reduce.8.cloned.1.call-start = ((), (), s32[]{:S(2)}) async-start(), calls=%async_computation.2 | async-start | bytes 2097152 | tf_op jit(solution)/shard_map/psum | solution.py:37
  281.1 492.9 %reduce-scatter.2.cloned.1.call-start = ((), (), s32[]{:S(2)}) async-start(), calls=%async_computation.3 | async-start | bytes 2228224 | tf_op jit(solution)/shard_map/reduce_scatter | solution.py:43
  423.8 1.7 copy-start.2
  425.7 1.0 copy-start.3
  485.9 83.5 %copy-start.1 = (f32[256,512]{0,1:T(8,128)S(1)}, f32[256,512]{0,1:T(8,128)}, u32[]{:S(2)}) copy-start(f32[256,512]{0,1:T(8,128)} %all-reduce.6.cloned.1.call-done) | copy-start | bytes 1572868
  709.3 64.7 %copy-start.7 = (f32[32,924]{1,0:T(8,128)S(1)}, f32[32,924]{1,0:T(8,128)}, u32[]{:S(2)}) copy-start(f32[32,924]{1,0:T(8,128)} %param.8) | copy-start | bytes 354820
  709.3 64.7 %copy-start.8 = (f32[32,924]{1,0:T(8,128)S(1)}, f32[32,924]{1,0:T(8,128)}, u32[]{:S(2)}) copy-start(f32[32,924]{1,0:T(8,128)} %param.9) | copy-start | bytes 354820
  775.6 0.7 copy-start.5
  775.6 0.7 copy-start.6
Sparse Core Ops, SparseCore 0:
  146.8 131.0 all-reduce.5
  282.0 141.7 all-reduce.7
  709.5 64.4 reduce-scatter.1
where the time goes:
time: 931 us; the launch traced here: 930 us
  blocking collectives  439 us (47%)
  waiting for transfers between devices  311 us (33%)
  other arithmetic  122 us (13%)
  local copies, waits for them, and re-layouts  20.5 us (2%)
  matrix products  19.8 us (2%)
  between operations  17.3 us (2%)
    psum x1, waiting for transfers between devices, shards(): gram_matrix = lax.psum(gram_local, 'mp')  142 us
    psum x1, blocking collectives, shards(): sketch_in = lax.psum(partial_in, 'mp').astype(jnp.bfloat16)  135 us
    psum x1, blocking collectives, shards(): coords = lax.psum(partial_coords, 'mp').astype(jnp.bfloat16)  133 us
    psum x1, waiting for transfers between devices, shards(): sketch = lax.psum(local_sketch, 'dp')  131 us
    psum x1, blocking collectives, shards(): total_squares = lax.psum(squares, ('dp', 'mp'))  117 us
    another operation x14, other arithmetic, orthonormal(): lower_factor = jnp.linalg.cholesky(gram_matrix)  78.6 us
    another operation x4, other arithmetic, orthonormal(): lax.linalg.triangular_solve(lower_factor, rows_block, left_side=False, lo...  41.5 us
    reduce_scatter x1, waiting for transfers between devices, shards(): lax.psum_scatter(jnp.einsum('tr,tf->rf', columns, out_grads, preferred_el...  37 us
  transfers between devices with their start and end apart: 3, of which 3 were waited for; matrix products, arithmetic and copies ran while one was open for 0% of the time, Pallas kernels for 0%

commit v1 on v0

v1 whole, which is shorter than its diff:
```python
import jax
import jax.numpy as jnp
from jax import lax
from jax.experimental import pallas as pl
from jax.experimental.pallas import tpu as pltpu
from jax.sharding import PartitionSpec as P

FF = 29568
R = 512
STEP = 100

beta_one = 0.9
beta_two = 0.999
adam_eps = 1e-08
norm_eps = 1e-06

MESH = pl.DeviceIdType.MESH
F32 = jnp.float32
BF16 = jnp.bfloat16
CHIPS = 16
DP = 16


def place():
    mp = lax.axis_index("mp")
    core = mp % 2
    chip = mp // 2
    return lax.axis_index("dp"), mp, chip, core


def chip_at(chip, k):
    x = (chip // 4 + k // 4) % 4
    y = (chip % 4 + k % 4) % 4
    return x * 4 + y


def greet(dp_offsets):
    dp, mp, chip, core = place()
    barrier = pltpu.get_barrier_semaphore()
    pl.semaphore_signal(barrier, inc=1, device_id={"mp": chip * 2 + 1 - core}, device_id_type=MESH)

    def to_chip(k, _):
        pl.semaphore_signal(
            barrier, inc=1, device_id={"mp": chip_at(chip, k) * 2 + core}, device_id_type=MESH
        )
        return 0

    lax.fori_loop(1, CHIPS, to_chip, 0)

    def to_ring(k, _):
        pl.semaphore_signal(barrier, inc=1, device_id={"dp": (dp + k) % DP}, device_id_type=MESH)
        return 0

    if dp_offsets == "all":
        lax.fori_loop(1, DP, to_ring, 0)
        return barrier, 1 + (CHIPS - 1) + (DP - 1)
    to_ring(1, 0)
    to_ring(DP - 1, 0)
    return barrier, 1 + (CHIPS - 1) + 2


def send(src, dst, sends, recvs, where):
    return pltpu.make_async_remote_copy(
        src_ref=src, dst_ref=dst, send_sem=sends, recv_sem=recvs, device_id=where, device_id_type=MESH
    )


def plane_scatter(stage, landed, sends, recvs):
    _, _, chip, core = place()

    def copy(k):
        there = chip_at(chip, k)
        return send(
            stage.at[there], landed.at[k - 1], sends.at[k - 1], recvs.at[k - 1], {"mp": there * 2 + core}
        )

    def go(k, _):
        copy(k).start()
        return 0

    lax.fori_loop(1, CHIPS, go, 0)
    return copy


def plane_gather(block, sends, recvs):
    _, _, chip, core = place()

    def copy(k):
        there = chip_at(chip, k)
        return send(block, block, sends.at[k - 1], recvs.at[k - 1], {"mp": there * 2 + core})

    def go(k, _):
        copy(k).start()
        return 0

    lax.fori_loop(1, CHIPS, go, 0)
    return copy


def wait_all(copy, first, last, recv=True):
    def step(k, _):
        if recv:
            copy(k).wait_recv()
        else:
            copy(k).wait_send()
        return 0

    lax.fori_loop(first, last, step, 0)


class PlaneSum:
    def scratch(kind):
        return [
            pltpu.VMEM((256, R), kind),
            pltpu.VMEM((256, R), kind),
            pltpu.VMEM((CHIPS, 16, R), kind),
            pltpu.VMEM((CHIPS - 1, 16, R), kind),
            pltpu.SemaphoreType.DMA((4,)),
            pltpu.SemaphoreType.DMA((CHIPS - 1,)),
            pltpu.SemaphoreType.DMA((CHIPS - 1,)),
            pltpu.SemaphoreType.DMA((CHIPS - 1,)),
            pltpu.SemaphoreType.DMA((CHIPS - 1,)),
        ]

    def run(half_of, full, kind, refs, between=None):
        give, take, stage, landed, pair_sems, s1, r1, s2, r2 = refs
        dp, mp, chip, core = place()
        partner = {"mp": chip * 2 + 1 - core}
        give[...] = half_of(1 - core).astype(kind)
        swap = send(give, take, pair_sems.at[0], pair_sems.at[1], partner)
        swap.start()
        own = half_of(core)
        swap.wait_recv()
        stage[...] = (own + take[...].astype(F32)).astype(kind).reshape(CHIPS, 16, R)
        scatter = plane_scatter(stage, landed, s1, r1)

        def add(k, total):
            scatter(k).wait_recv()
            return total + landed[k - 1].astype(F32)

        total = lax.fori_loop(1, CHIPS, add, stage[chip].astype(F32))
        mine = pl.ds(pl.multiple_of(core * 256 + chip * 16, 16), 16)
        full[mine, :] = total.astype(kind)
        gather = plane_gather(full.at[mine, :], s2, r2)
        wait_all(gather, 1, CHIPS)
        half = full.at[pl.ds(pl.multiple_of(core * 256, 256), 256), :]
        swap_full = send(half, half, pair_sems.at[2], pair_sems.at[3], partner)
        swap_full.start()
        if between is not None:
            between()
        swap_full.wait_recv()

        def finish():
            swap.wait_send()
            wait_all(scatter, 1, CHIPS, recv=False)
            wait_all(gather, 1, CHIPS, recv=False)
            swap_full.wait_send()

        return finish


class Ring:
    RIGHT, LEFT = 8, 7

    def scratch_scatter(rows, width, parts):
        return [
            pltpu.VMEM((Ring.RIGHT, rows, width), BF16),
            pltpu.VMEM((Ring.RIGHT, rows, width), BF16),
            pltpu.VMEM((Ring.LEFT, rows, width), BF16),
            pltpu.VMEM((Ring.LEFT, rows, width), BF16),
            pltpu.SemaphoreType.DMA((Ring.RIGHT, parts)),
            pltpu.SemaphoreType.DMA((Ring.RIGHT, parts)),
            pltpu.SemaphoreType.DMA((Ring.LEFT, parts)),
            pltpu.SemaphoreType.DMA((Ring.LEFT, parts)),
        ]

    def scratch_gather(parts):
        return [
            pltpu.SemaphoreType.DMA((Ring.RIGHT, parts)),
            pltpu.SemaphoreType.DMA((Ring.RIGHT, parts)),
            pltpu.SemaphoreType.DMA((Ring.LEFT, parts)),
            pltpu.SemaphoreType.DMA((Ring.LEFT, parts)),
        ]

    def reduce_scatter(local, refs, rows, parts, put):
        give_r, take_r, give_l, take_l, sr, rr, sl, rl = refs
        dp, _, _, _ = place()
        right, left = {"dp": (dp + 1) % DP}, {"dp": (dp + DP - 1) % DP}
        piece = rows // parts

        def cut(p):
            return pl.ds(p * piece, piece)

        def copy_r(s, p):
            return send(
                give_r.at[s, cut(p)], take_r.at[s, cut(p)], sr.at[s, p], rr.at[s, p], right
            )

        def copy_l(s, p):
            return send(
                give_l.at[s, cut(p)], take_l.at[s, cut(p)], sl.at[s, p], rl.at[s, p], left
            )

        for p in range(parts):
            give_r[0, cut(p)] = local[(dp + 8) % DP, cut(p)].astype(BF16)
            copy_r(0, p).start()
            give_l[0, cut(p)] = local[(dp + 9) % DP, cut(p)].astype(BF16)
            copy_l(0, p).start()

        def step_r(s, p):
            copy_r(s - 1, p).wait_recv()
            held = take_r[s - 1, cut(p)].astype(F32)
            give_r[s, cut(p)] = (held + local[(dp + 8 + DP - s) % DP, cut(p)]).astype(BF16)
            copy_r(s, p).start()

        def step_l(s, p):
            copy_l(s - 1, p).wait_recv()
            held = take_l[s - 1, cut(p)].astype(F32)
            give_l[s, cut(p)] = (held + local[(dp + 9 + s) % DP, cut(p)]).astype(BF16)
            copy_l(s, p).start()

        def step(s, _):
            for p in range(parts):
                step_r(s, p)
                step_l(s, p)
            return 0

        lax.fori_loop(1, Ring.LEFT, step, 0)
        for p in range(parts):
            step_r(Ring.LEFT, p)
        for p in range(parts):
            copy_l(Ring.LEFT - 1, p).wait_recv()
            copy_r(Ring.RIGHT - 1, p).wait_recv()
            both = take_l[Ring.LEFT - 1, cut(p)].astype(F32) + take_r[Ring.RIGHT - 1, cut(p)].astype(F32)
            put(cut(p), both + local[dp, cut(p)])

        def finish():
            def drain_r(s, _):
                for p in range(parts):
                    copy_r(s, p).wait_send()
                return 0

            def drain_l(s, _):
                for p in range(parts):
                    copy_l(s, p).wait_send()
                return 0

            lax.fori_loop(0, Ring.RIGHT, drain_r, 0)
            lax.fori_loop(0, Ring.LEFT, drain_l, 0)

        return finish

    def all_gather(whole, refs, rows, parts, between=()):
        sr, rr, sl, rl = refs
        dp, _, _, _ = place()
        right, left = {"dp": (dp + 1) % DP}, {"dp": (dp + DP - 1) % DP}
        piece = rows // parts

        def copy_r(s, p):
            part = whole.at[(dp + DP - s) % DP, pl.ds(p * piece, piece)]
            return send(part, part, sr.at[s, p], rr.at[s, p], right)

        def copy_l(s, p):
            part = whole.at[(dp + s) % DP, pl.ds(p * piece, piece)]
            return send(part, part, sl.at[s, p], rl.at[s, p], left)

        for p in range(parts):
            copy_r(0, p).start()
            copy_l(0, p).start()
        for s in range(1, Ring.RIGHT):
            for p in range(parts):
                copy_r(s - 1, p).wait_recv()
                copy_r(s, p).start()
                copy_l(s - 1, p).wait_recv()
                if s < Ring.LEFT:
                    copy_l(s, p).start()
            if s - 1 < len(between):
                between[s - 1]()
        for p in range(parts):
            copy_r(Ring.RIGHT - 1, p).wait_recv()

        def finish():
            def drain_r(s, _):
                for p in range(parts):
                    copy_r(s, p).wait_send()
                return 0

            def drain_l(s, _):
                for p in range(parts):
                    copy_l(s, p).wait_send()
                return 0

            lax.fori_loop(0, Ring.RIGHT, drain_r, 0)
            lax.fori_loop(0, Ring.LEFT, drain_l, 0)

        return finish


def half_rows(h):
    return pl.ds(pl.multiple_of(h * 256, 256), 256)


def dot_t(a, b):
    return lax.dot_general(a, b, (((0,), (0,)), ((), ())), preferred_element_type=F32)


N_PLANE = 9
N_SCATTER = 8
N_GATHER = 4


def sketch_kernel(og, tm, act, sketch, gram, *refs):
    plane_one = refs[:N_PLANE]
    plane_two = refs[N_PLANE : 2 * N_PLANE]
    rest = refs[2 * N_PLANE :]
    scatter, gather = rest[:N_SCATTER], rest[N_SCATTER : N_SCATTER + N_GATHER]
    sketch_in, local, gram_local = rest[N_SCATTER + N_GATHER :]
    dp, mp, chip, core = place()
    barrier, count = greet("ends")
    pl.semaphore_wait(barrier, count)

    def in_half(h):
        return jnp.dot(og[half_rows(h), :], tm[...], preferred_element_type=F32)

    def near_half():
        local[...] = dot_t(act[half_rows(core), :], sketch_in[half_rows(core), :]).reshape(DP, 16, R)

    done_one = PlaneSum.run(in_half, sketch_in, BF16, plane_one, near_half)
    far = half_rows(1 - core)
    local[...] += dot_t(act[far, :], sketch_in[far, :]).reshape(DP, 16, R)

    def put(rows, total):
        sketch[dp, rows] = total.astype(BF16)

    done_scatter = Ring.reduce_scatter(local, scatter, 16, 1, put)
    done_gather = Ring.all_gather(sketch, gather, 16, 1)
    rows_block = sketch[...].reshape(256, R)
    gram_local[...] = dot_t(rows_block, rows_block)

    def gram_half(h):
        return gram_local[half_rows(h), :]

    done_two = PlaneSum.run(gram_half, gram, F32, plane_two)
    done_one()
    done_scatter()
    done_gather()
    done_two()


VMEM = pl.BlockSpec(memory_space=pltpu.VMEM)


def sketch_call(out_grads, test_matrix, activations):
    return pl.pallas_call(
        sketch_kernel,
        out_shape=(
            jax.ShapeDtypeStruct((DP, 16, R), BF16),
            jax.ShapeDtypeStruct((R, R), F32),
        ),
        in_specs=[VMEM] * 3,
        out_specs=(VMEM, VMEM),
        scratch_shapes=[
            *PlaneSum.scratch(BF16),
            *PlaneSum.scratch(F32),
            *Ring.scratch_scatter(16, R, 1),
            *Ring.scratch_gather(1),
            pltpu.VMEM((R, R), BF16),
            pltpu.VMEM((DP, 16, R), F32),
            pltpu.VMEM((R, R), F32),
        ],
        compiler_params=pltpu.CompilerParams(
            collective_id=0, has_side_effects=True, vmem_limit_bytes=40 * 2**20
        ),
        name="sketch_and_gram",
    )(out_grads, test_matrix, activations)


def adam_kernel(act, basis, og, first, second, update, new_first, new_second, *refs):
    plane = refs[:N_PLANE]
    rest = refs[N_PLANE:]
    scatter, gather = rest[:N_SCATTER], rest[N_SCATTER : N_SCATTER + N_GATHER]
    rest = rest[N_SCATTER + N_GATHER :]
    coords, local, whole, slots, ss, sr, slot_pair, tiles, landed, sq_pair, qs, qr, zs, zr = rest
    dp, mp, chip, core = place()
    partner = {"mp": chip * 2 + 1 - core}
    barrier, count = greet("all")
    pl.semaphore_wait(barrier, count)

    def coords_half(h):
        return jnp.dot(act[half_rows(h), :], basis[...], preferred_element_type=F32)

    done_plane = PlaneSum.run(coords_half, coords, BF16, plane)

    slots[chip, core] = basis[pl.ds(pl.multiple_of(dp * 16, 16), 16), :]
    slot_gather = plane_gather(slots.at[chip, core], ss, sr)

    local[...] = dot_t(coords[...], og[...]).reshape(DP, 32, og.shape[1])
    squares = []

    def put(rows, projected):
        new_m = beta_one * first[rows, :] + (1.0 - beta_one) * projected
        new_v = beta_two * second[rows, :] + (1.0 - beta_two) * projected * projected
        new_first[rows, :] = new_m
        new_second[rows, :] = new_v
        correct_one = 1.0 - beta_one**STEP
        correct_two = 1.0 - beta_two**STEP
        direction = new_m / correct_one / (jnp.sqrt(new_v / correct_two) + adam_eps)
        squares.append(jnp.sum(direction * direction, keepdims=True))
        whole[dp, rows] = direction.astype(BF16)

    done_scatter = Ring.reduce_scatter(local, scatter, 32, 2, put)

    pair_copy = send(tiles.at[0], landed.at[0], sq_pair.at[0], sq_pair.at[1], partner)

    def chip_copy(k):
        return send(
            tiles.at[1], landed.at[k], qs.at[k - 1], qr.at[k - 1], {"mp": chip_at(chip, k) * 2 + core}
        )

    def plane_copy(k):
        return send(
            tiles.at[2], landed.at[15 + k], zs.at[k - 1], zr.at[k - 1], {"dp": (dp + k) % DP}
        )

    def start_all(copy):
        def go(k, _):
            copy(k).start()
            return 0

        lax.fori_loop(1, 16, go, 0)

    def add_all(copy, base, total):
        def go(k, value):
            copy(k).wait_recv()
            return value + landed[base + k]

        return lax.fori_loop(1, 16, go, total)

    slot_half = slots.at[:, core]
    slot_swap = send(slot_half, slot_half, slot_pair.at[0], slot_pair.at[1], partner)

    def after_one():
        pair_copy.wait_recv()
        tiles[1] = tiles[0] + landed[0]
        start_all(chip_copy)

    def after_two():
        wait_all(slot_gather, 1, CHIPS)
        slot_swap.start()

    def after_three():
        tiles[2] = add_all(chip_copy, 0, tiles[1])
        start_all(plane_copy)

    tiles[0] = jnp.broadcast_to(sum(squares), (8, 128))
    pair_copy.start()
    done_gather = Ring.all_gather(whole, gather, 32, 2, (after_one, after_two, after_three))
    slot_swap.wait_recv()
    total_squares = add_all(plane_copy, 15, tiles[2])
    factor = lax.rsqrt(total_squares / (R * FF) + norm_eps)[0:1, 0:1]
    rows_of = slots[...].reshape(R, R)
    product = jnp.dot(rows_of, whole[...].reshape(R, og.shape[1]), preferred_element_type=F32)
    update[...] = (factor * product).astype(BF16)

    done_plane()
    done_scatter()
    done_gather()
    wait_all(slot_gather, 1, CHIPS, recv=False)
    slot_swap.wait_send()
    pair_copy.wait_send()
    wait_all(chip_copy, 1, 16, recv=False)
    wait_all(plane_copy, 1, 16, recv=False)


def adam_call(activations, basis, out_grads, first, second):
    width = out_grads.shape[1]
    return pl.pallas_call(
        adam_kernel,
        out_shape=(
            jax.ShapeDtypeStruct((R, width), BF16),
            jax.ShapeDtypeStruct(first.shape, F32),
            jax.ShapeDtypeStruct(second.shape, F32),
        ),
        in_specs=[VMEM] * 5,
        out_specs=(VMEM,) * 3,
        scratch_shapes=[
            *PlaneSum.scratch(BF16),
            *Ring.scratch_scatter(32, width, 2),
            *Ring.scratch_gather(2),
            pltpu.VMEM((R, R), BF16),
            pltpu.VMEM((DP, 32, width), F32),
            pltpu.VMEM((DP, 32, width), BF16),
            pltpu.VMEM((CHIPS, 2, 16, R), BF16),
            pltpu.SemaphoreType.DMA((CHIPS - 1,)),
            pltpu.SemaphoreType.DMA((CHIPS - 1,)),
            pltpu.SemaphoreType.DMA((2,)),
            pltpu.VMEM((3, 8, 128), F32),
            pltpu.VMEM((31, 8, 128), F32),
            pltpu.SemaphoreType.DMA((2,)),
            pltpu.SemaphoreType.DMA((15,)),
            pltpu.SemaphoreType.DMA((15,)),
            pltpu.SemaphoreType.DMA((15,)),
            pltpu.SemaphoreType.DMA((15,)),
        ],
        compiler_params=pltpu.CompilerParams(
            collective_id=1, has_side_effects=True, vmem_limit_bytes=40 * 2**20
        ),
        name="project_and_update",
    )(activations, basis, out_grads, first, second)


def orthonormal(rows_block, gram_matrix):
    lower_factor = jnp.linalg.cholesky(gram_matrix)
    return lax.linalg.triangular_solve(
        lower_factor, rows_block, left_side=False, lower=True, transpose_a=True
    )


def shards(activations, out_grads, test_matrix, first_moment, second_moment):
    sketch, gram_matrix = sketch_call(out_grads, test_matrix, activations)
    rows_block = sketch.reshape(activations.shape[1], R).astype(F32)
    basis_b = orthonormal(rows_block, gram_matrix).astype(BF16)
    update, new_first, new_second = adam_call(
        activations, basis_b, out_grads, first_moment, second_moment
    )
    return (update.reshape(lax.axis_size("mp"), 16, out_grads.shape[1]), new_first, new_second)


def solution(mesh):
    placed = (P("dp", "mp"), P("dp", "mp"), P("mp", None), P("dp", "mp"), P("dp", "mp"))
    return jax.shard_map(
        shards,
        mesh=mesh,
        in_specs=placed,
        out_specs=(P(None, "dp", "mp"), P("dp", "mp"), P("dp", "mp")),
        check_vma=False,
    )
```

time: 931 us -> 337 us (0.36)
  the two profiles are of different devices: /device:TPU:1 before, /device:TPU:2 now
where the time goes in v1:
time: 337 us
  Pallas kernels  180 us (53%)
  other arithmetic  124 us (37%)
  local copies, waits for them, and re-layouts  20.2 us (6%)
  matrix products  9.24 us (3%)
  between operations  3.56 us (1%)
    pallas_call x1, Pallas kernels, sketch_call(): pl.pallas_call(sketch_kernel, out_shape=(jax.ShapeDtypeStruct((DP, 16, R)...  96.5 us
    pallas_call x1, Pallas kernels, adam_call(): pl.pallas_call(adam_kernel, out_shape=(jax.ShapeDtypeStruct((R, width), B...  83.5 us
    another operation x14, other arithmetic, orthonormal(): lower_factor = jnp.linalg.cholesky(gram_matrix)  83 us
    another operation x4, other arithmetic, orthonormal(): lax.linalg.triangular_solve(lower_factor, rows_block, left_side=False, lo...  40.5 us
    another operation x12, local copies, waits for them, and re-layouts  11.6 us
    unnamed x22, local copies, waits for them, and re-layouts  7.11 us

profile of v1, /device:TPU:2, one launch (start us, length us, event | category | flops | bytes accessed | tf_op | source)
XLA Modules:
  0.0 336.7 jit_solution(7966710634521767882)
XLA Ops:
  0.7 1.6 copy.8.og
  2.3 96.5 %sketch_and_gram.1 = (bf16[16,16,512]{2,1,0:T(8,128)(2,1)S(1)}, f32[512,512]{1,0:T(8,128)S(1)}) custom-call(bf16[512,924]{1,0:T(8,128)(2,1)S(1)} %copy.8.og, bf16[924,512]{1,0:T(8,128)(2,1)S(1)} %copy-done.1, bf16[512,256]{1,0:T(8,128)(2,1)S(1)} %copy-done), custom_call_target="tpu_custom_call" | custom-call | tf_op jit(solution)/shard_map/sketch_and_gram/pallas_call | solution.py:354
  101.0 11.7 %cholesky.104 = f32[128,128]{1,0:T(8,128)S(1)} custom-call(f32[128,128]{1,0:T(8,128)S(1)} %cholesky.266), custom_call_target="Cholesky" | custom-call | tf_op jit(solution)/shard_map/jit(cholesky)/cholesky | solution.py:513
  112.7 9.8 %custom-call.30 = f32[1,128,128]{1,2,0:T(8,128)S(1)} custom-call(f32[1,128,128]{2,1,0:T(8,128)S(1)} %get-tuple-element.40), custom_call_target="InvertDiagBlocksLowerTriangular" | custom-call | tf_op jit(solution)/shard_map/jit(cholesky)/cholesky | solution.py:513
  124.0 11.7 %cholesky.217 = f32[128,128]{1,0:T(8,128)S(1)} custom-call(f32[128,128]{1,0:T(8,128)S(1)} %cholesky.270), custom_call_target="Cholesky" | custom-call | tf_op jit(solution)/shard_map/jit(cholesky)/cholesky | solution.py:513
  137.7 9.9 %custom-call.31 = f32[1,128,128]{1,2,0:T(8,128)S(1)} custom-call(f32[1,128,128]{2,1,0:T(8,128)S(1)} %get-tuple-element.37), custom_call_target="InvertDiagBlocksLowerTriangular" | custom-call | tf_op jit(solution)/shard_map/jit(cholesky)/cholesky | solution.py:513
  147.7 1.2 convolution_dynamic-update-slice_fusion
  149.9 13.2 %cholesky.238 = f32[128,128]{1,0:T(8,128)} custom-call(f32[128,128]{1,0:T(8,128)} %cholesky.275), custom_call_target="Cholesky" | custom-call | tf_op jit(solution)/shard_map/jit(cholesky)/cholesky | solution.py:513
  163.0 1.5 select_reduce_fusion.1
  165.8 11.3 %custom-call.32 = f32[1,128,128]{1,2,0:T(8,128)} custom-call(f32[1,128,128]{2,1,0:T(8,128)} %get-tuple-element.34), custom_call_target="InvertDiagBlocksLowerTriangular" | custom-call | tf_op jit(solution)/shard_map/jit(cholesky)/cholesky | solution.py:513
  177.1 1.0 convolution_dynamic-update-slice_fusion.1
  178.5 11.9 %cholesky.255 = f32[128,128]{1,0:T(8,128)S(1)} custom-call(f32[128,128]{1,0:T(8,128)S(1)} %convolution_subtract_fusion.5), custom_call_target="Cholesky" | custom-call | tf_op jit(solution)/shard_map/jit(cholesky)/cholesky | solution.py:513
  191.7 1.1 select_select_fusion
  192.9 11.7 %while.1 = (s32[]{:T(128)}, f32[512,512]{1,0:T(8,128)}, s32[4,2]{0,1:T(2,128)S(1)}, f32[4,128,128]{2,1,0:T(8,128)S(1)}, s32[]{:T(128)}) while((s32[]{:T(128)}, f32[512,512]{1,0:T(8,128)}, s32[4,2]{0,1:T(2,128)S(1)}, f32[4,128,128]{2,1,0:T(8,128)S(1)}, s32[]{:T(128)}) %tuple.31), condition=%wide.while_cond, body=%wide.while_body.sunk | while | flops 2 | bytes 131181 | solution.py:514
  193.5 2.3 bitcast_dynamic-update-slice_fusion.2
  196.4 2.3 bitcast_dynamic-update-slice_fusion.2
  199.4 2.3 bitcast_dynamic-update-slice_fusion.2
  202.3 2.2 bitcast_dynamic-update-slice_fusion.2
  204.5 39.3 %custom-call.33 = f32[4,128,128]{1,2,0:T(8,128)S(1)} custom-call(f32[4,128,128]{2,1,0:T(8,128)S(1)} %get-tuple-element.20), custom_call_target="InvertDiagBlocksLowerTriangular" | custom-call | tf_op jit(solution)/shard_map/triangular_solve | solution.py:514
  244.2 1.2 convolution_subtract_fusion.4
  245.8 1.5 convolution_subtract_fusion.2
  247.6 1.8 convolution_subtract_fusion.1
  251.0 83.5 %project_and_update.1 = (bf16[512,924]{1,0:T(8,128)(2,1)S(1)}, f32[32,924]{1,0:T(8,128)S(1)}, f32[32,924]{1,0:T(8,128)S(1)}) custom-call(bf16[512,256]{1,0:T(8,128)(2,1)S(1)} %copy-done, bf16[256,512]{1,0:T(8,128)(2,1)S(1)} %pad_maximum_fusion.basis, bf16[512,924]{1,0:T(8,128)(2,1)S(1)} %copy.8.og, f32[32,924]{1,0:T(8,128)S(1)} %copy-done.4, ...), custom_call_target="tpu_custom_call" | custom-call | tf_op jit(solution)/shard_map/project_and_update/pallas_call | solution.py:477
  334.4 1.0 copy.34
  (56 shorter events, 13.5 us)
Async XLA Ops:
  0.6 1.6 copy-start
  0.6 1.6 copy-start.1
  98.7 0.7 copy-start.2
  100.0 1.0 copy-start.6
  101.0 21.7 %copy-start.7 = (f32[512,512]{1,0:T(8,128)S(1)}, f32[512,512]{1,0:T(8,128)}, u32[]{:S(2)}) copy-start(f32[512,512]{1,0:T(8,128)} %copy-done.6) | copy-start | bytes 3145732
  123.3 0.7 copy-start.8
  191.7 52.1 %copy-start.3 = (bf16[16,16,512]{2,1,0:T(8,128)(2,1)S(1)}, bf16[16,16,512]{2,1,0:T(8,128)(2,1)}, u32[]{:S(2)}) copy-start(bf16[16,16,512]{2,1,0:T(8,128)(2,1)} %copy-done.2) | copy-start | bytes 786436
  250.0 0.9 copy-start.4
  250.0 1.0 copy-start.5

commit v2 on v1

--- a/solution.py
+++ b/solution.py
@@ -509,17 +509,78 @@
     )(activations, basis, out_grads, first, second)
 
 
-def orthonormal(rows_block, gram_matrix):
-    lower_factor = jnp.linalg.cholesky(gram_matrix)
-    return lax.linalg.triangular_solve(
-        lower_factor, rows_block, left_side=False, lower=True, transpose_a=True
+LEAF = 128
+
+
+def exact_dot(a, b, dims):
+    return lax.dot_general(
+        a, b, (dims, ((), ())), precision=lax.Precision.HIGHEST, preferred_element_type=F32
     )
+
+
+def leaf_inverse(block, inverse):
+    groups = LEAF // 8
+    sub = lax.broadcasted_iota(jnp.int32, (8, 128), 0)
+
+    def spread(row):
+        return jnp.broadcast_to(row, (8, 128))
+
+    for p in range(groups):
+        cols = {
+            g: [spread(block[g][:, 8 * p + j : 8 * p + j + 1]) for j in range(8)]
+            for g in range(p, groups)
+        }
+        pivots = jnp.zeros((8, 128), F32)
+        for j in range(8):
+            pivot = spread(cols[p][j][j : j + 1, :])
+            over = 1.0 / pivot
+            pivots = jnp.where(sub == j, pivot, pivots)
+            below = jnp.where(sub > j, cols[p][j], 0.0)
+            row_block = spread(block[p][j : j + 1, :]) * over
+            row_inverse = spread(inverse[p][j : j + 1, :]) * over
+            ratio = {i: spread(cols[p][j][i : i + 1, :]) * over for i in range(j + 1, 8)}
+            for g in range(p, groups):
+                left = below if g == p else cols[g][j]
+                for i in range(j + 1, 8):
+                    cols[g][i] = cols[g][i] - left * ratio[i]
+                block[g] = block[g] - left * row_block
+                inverse[g] = inverse[g] - left * row_inverse
+        inverse[p] = inverse[p] * lax.rsqrt(pivots)
+    return jnp.concatenate(inverse, axis=0)
+
+
+def basis_kernel(gram, sketch, basis, whole):
+    whole[:, :R] = gram[...]
+    whole[:, R:] = sketch[...].astype(F32).T
+    lane = lax.broadcasted_iota(jnp.int32, (8, 128), 1)
+    sub = lax.broadcasted_iota(jnp.int32, (8, 128), 0)
+    for k in range(R // LEAF):
+        here, after = k * LEAF, (k + 1) * LEAF
+        block = [whole[here + 8 * g : here + 8 * g + 8, here:after] for g in range(LEAF // 8)]
+        unit = [jnp.where(lane == sub + 8 * g, 1.0, 0.0) for g in range(LEAF // 8)]
+        inverse = leaf_inverse(block, unit)
+        panel = exact_dot(inverse, whole[here:after, after:], ((1,), (0,)))
+        tail = R - after
+        if tail:
+            whole[after:, after:] -= exact_dot(panel[:, :tail], panel, ((0,), (0,)))
+        basis[:, here:after] = panel[:, tail:].T.astype(BF16)
+
+
+def basis_call(gram_matrix, sketch):
+    return pl.pallas_call(
+        basis_kernel,
+        out_shape=jax.ShapeDtypeStruct(sketch.shape, BF16),
+        in_specs=[VMEM] * 2,
+        out_specs=VMEM,
+        scratch_shapes=[pltpu.VMEM((R, R + sketch.shape[0]), F32)],
+        compiler_params=pltpu.CompilerParams(vmem_limit_bytes=40 * 2**20),
+        name="orthonormal",
+    )(gram_matrix, sketch)
 
 
 def shards(activations, out_grads, test_matrix, first_moment, second_moment):
     sketch, gram_matrix = sketch_call(out_grads, test_matrix, activations)
-    rows_block = sketch.reshape(activations.shape[1], R).astype(F32)
-    basis_b = orthonormal(rows_block, gram_matrix).astype(BF16)
+    basis_b = basis_call(gram_matrix, sketch.reshape(activations.shape[1], R))
     update, new_first, new_second = adam_call(
         activations, basis_b, out_grads, first_moment, second_moment
     )

time: 337 us -> 205 us (0.61)
  other arithmetic: 124 us -> 0 us
  Pallas kernels: 180 us -> 200 us
  local copies, waits for them, and re-layouts: 20.2 us -> 3.88 us
  matrix products: 9.24 us -> 0 us
    another operation x18 -> x0, other arithmetic: 123 us -> none  [the longest x14 83 us: orthonormal(): lower_factor = jnp.linalg.cholesky(gram_matrix)]
    pallas_call x0 -> x1, Pallas kernels: none -> 19.6 us  [basis_call(): pl.pallas_call(basis_kernel, out_shape=jax.ShapeDtypeStruct(sketch.shape,...]
    another operation x20 -> x0, local copies, waits for them, and re-layouts: 12.7 us -> none
    another operation x13 -> x0, matrix products: 9.24 us -> none  [the longest x7 5.63 us: orthonormal(): lax.linalg.triangular_solve(lower_factor, rows_block, left_side=False, lo...]
    unnamed x22 -> x12, local copies, waits for them, and re-layouts: 7.11 us -> 3.88 us
where the time goes in v2:
time: 205 us; the launch traced here: 204 us
  Pallas kernels  200 us (98%)
  local copies, waits for them, and re-layouts  3.88 us (2%)
    pallas_call x1, Pallas kernels, sketch_call(): pl.pallas_call(sketch_kernel, out_shape=(jax.ShapeDtypeStruct((DP, 16, R)...  96.5 us
    pallas_call x1, Pallas kernels, adam_call(): pl.pallas_call(adam_kernel, out_shape=(jax.ShapeDtypeStruct((R, width), B...  83.7 us
    pallas_call x1, Pallas kernels, basis_call(): pl.pallas_call(basis_kernel, out_shape=jax.ShapeDtypeStruct(sketch.shape,...  19.6 us

profile of v2, /device:TPU:2, one launch (start us, length us, event | category | flops | bytes accessed | tf_op | source)
XLA Modules:
  0.0 204.4 jit_solution(4634300109393306319)
XLA Ops:
  0.6 0.0 copy-start
  0.6 0.0 copy-start.1
  0.7 1.6 copy.8.og
  2.2 0.0 copy-done
  2.2 0.0 copy-done.1
  2.3 96.5 %sketch_and_gram.1 = (bf16[16,16,512]{2,1,0:T(8,128)(2,1)S(1)}, f32[512,512]{1,0:T(8,128)S(1)}) custom-call(bf16[512,924]{1,0:T(8,128)(2,1)S(1)} %copy.8.og, bf16[924,512]{1,0:T(8,128)(2,1)S(1)} %copy-done.1, bf16[512,256]{1,0:T(8,128)(2,1)S(1)} %copy-done), custom_call_target="tpu_custom_call" | custom-call | tf_op jit(solution)/shard_map/sketch_and_gram/pallas_call | solution.py:354
  98.7 0.0 copy-start.2
  98.7 0.0 copy-start.3
  98.8 19.6 %orthonormal.1.basis = bf16[256,512]{1,0:T(8,128)(2,1)S(1)} custom-call(f32[512,512]{1,0:T(8,128)S(1)} %get-tuple-element.8.gram, bf16[256,512]{1,0:T(8,128)(2,1)S(1)} %bitcast.3), custom_call_target="tpu_custom_call" | custom-call | tf_op jit(solution)/shard_map/orthonormal/pallas_call | solution.py:570
  118.3 0.0 copy-done.2
  118.4 0.0 copy-done.3
  118.4 83.7 %project_and_update.1 = (bf16[512,924]{1,0:T(8,128)(2,1)S(1)}, f32[32,924]{1,0:T(8,128)S(1)}, f32[32,924]{1,0:T(8,128)S(1)}) custom-call(bf16[512,256]{1,0:T(8,128)(2,1)S(1)} %copy-done, bf16[256,512]{1,0:T(8,128)(2,1)S(1)} %orthonormal.1.basis, bf16[512,924]{1,0:T(8,128)(2,1)S(1)} %copy.8.og, f32[32,924]{1,0:T(8,128)S(1)} %copy-done.2, f32[32,924]{1,0:T(8,128)S(1)} %copy-done.3), custom_call_target="tpu_custom_call" | custom-call | tf_op jit(solution)/shard_map/project_and_update/pallas_call | solution.py:477
  202.1 1.0 copy.13
  203.1 0.7 copy.14
  203.7 0.7 copy.15
Async XLA Ops:
  0.6 1.6 copy-start
  0.6 1.6 copy-start.1
  98.7 19.6 %copy-start.2 = (f32[32,924]{1,0:T(8,128)S(1)}, f32[32,924]{1,0:T(8,128)}, u32[]{:S(2)}) copy-start(f32[32,924]{1,0:T(8,128)} %first.1) | copy-start | bytes 354820
  98.7 19.6 %copy-start.3 = (f32[32,924]{1,0:T(8,128)S(1)}, f32[32,924]{1,0:T(8,128)}, u32[]{:S(2)}) copy-start(f32[32,924]{1,0:T(8,128)} %second.1) | copy-start | bytes 354820

commit v3 on v0

v3 whole, which is shorter than its diff:
```python
import jax
import jax.numpy as jnp
from jax import lax
from jax.experimental import pallas as pl
from jax.experimental.pallas import tpu as pltpu
from jax.sharding import PartitionSpec as P

FF = 29568
R = 512
STEP = 100

beta_one = 0.9
beta_two = 0.999
adam_eps = 1e-08
norm_eps = 1e-06

MESH = pl.DeviceIdType.MESH
F32 = jnp.float32
BF16 = jnp.bfloat16
CHIPS = 16
DP = 16


def place():
    mp = lax.axis_index("mp")
    core = mp % 2
    chip = mp // 2
    return lax.axis_index("dp"), mp, chip, core


def chip_at(chip, k):
    x = (chip // 4 + k // 4) % 4
    y = (chip % 4 + k % 4) % 4
    return x * 4 + y


def greet(dp_offsets):
    dp, mp, chip, core = place()
    barrier = pltpu.get_barrier_semaphore()
    pl.semaphore_signal(barrier, inc=1, device_id={"mp": chip * 2 + 1 - core}, device_id_type=MESH)

    def to_chip(k, _):
        pl.semaphore_signal(
            barrier, inc=1, device_id={"mp": chip_at(chip, k) * 2 + core}, device_id_type=MESH
        )
        return 0

    lax.fori_loop(1, CHIPS, to_chip, 0)

    def to_ring(k, _):
        pl.semaphore_signal(barrier, inc=1, device_id={"dp": (dp + k) % DP}, device_id_type=MESH)
        return 0

    if dp_offsets == "all":
        lax.fori_loop(1, DP, to_ring, 0)
        return barrier, 1 + (CHIPS - 1) + (DP - 1)
    to_ring(1, 0)
    to_ring(DP - 1, 0)
    return barrier, 1 + (CHIPS - 1) + 2


def send(src, dst, sends, recvs, where):
    return pltpu.make_async_remote_copy(
        src_ref=src, dst_ref=dst, send_sem=sends, recv_sem=recvs, device_id=where, device_id_type=MESH
    )


def plane_scatter(stage, landed, sends, recvs):
    _, _, chip, core = place()

    def copy(k):
        there = chip_at(chip, k)
        return send(
            stage.at[there], landed.at[k - 1], sends.at[k - 1], recvs.at[k - 1], {"mp": there * 2 + core}
        )

    def go(k, _):
        copy(k).start()
        return 0

    lax.fori_loop(1, CHIPS, go, 0)
    return copy


def plane_gather(block, sends, recvs):
    _, _, chip, core = place()

    def copy(k):
        there = chip_at(chip, k)
        return send(block, block, sends.at[k - 1], recvs.at[k - 1], {"mp": there * 2 + core})

    def go(k, _):
        copy(k).start()
        return 0

    lax.fori_loop(1, CHIPS, go, 0)
    return copy


def wait_all(copy, first, last, recv=True):
    def step(k, _):
        if recv:
            copy(k).wait_recv()
        else:
            copy(k).wait_send()
        return 0

    lax.fori_loop(first, last, step, 0)


class PlaneSum:
    COUNT = 9

    def scratch(kind):
        return [
            pltpu.VMEM((256, R), kind),
            pltpu.VMEM((256, R), kind),
            pltpu.VMEM((CHIPS, 16, R), kind),
            pltpu.VMEM((CHIPS - 1, 16, R), kind),
            pltpu.SemaphoreType.DMA((4,)),
            pltpu.SemaphoreType.DMA((CHIPS - 1,)),
            pltpu.SemaphoreType.DMA((CHIPS - 1,)),
            pltpu.SemaphoreType.DMA((CHIPS - 1,)),
            pltpu.SemaphoreType.DMA((CHIPS - 1,)),
        ]

    def __init__(self, half_of, full, kind, refs):
        self.half_of, self.full, self.kind = half_of, full, kind
        self.give, self.take, self.stage, self.landed, pair, self.s1, self.r1, self.s2, self.r2 = refs
        _, _, self.chip, self.core = place()
        partner = {"mp": self.chip * 2 + 1 - self.core}
        self.swap = send(self.give, self.take, pair.at[0], pair.at[1], partner)
        half = full.at[half_rows(self.core), :]
        self.swap_full = send(half, half, pair.at[2], pair.at[3], partner)

    def start(self):
        self.give[...] = self.half_of(1 - self.core).astype(self.kind)
        self.swap.start()

    def scatter(self):
        own = self.half_of(self.core)
        self.swap.wait_recv()
        both = own + self.take[...].astype(F32)
        self.stage[...] = both.astype(self.kind).reshape(CHIPS, 16, R)
        self.out = plane_scatter(self.stage, self.landed, self.s1, self.r1)

    def gather(self):
        def add(k, total):
            self.out(k).wait_recv()
            return total + self.landed[k - 1].astype(F32)

        total = lax.fori_loop(1, CHIPS, add, self.stage[self.chip].astype(F32))
        mine = pl.ds(pl.multiple_of(self.core * 256 + self.chip * 16, 16), 16)
        self.full[mine, :] = total.astype(self.kind)
        self.back = plane_gather(self.full.at[mine, :], self.s2, self.r2)

    def share(self):
        wait_all(self.back, 1, CHIPS)
        self.swap_full.start()

    def end(self):
        self.swap_full.wait_recv()

    def drain(self):
        self.swap.wait_send()
        wait_all(self.out, 1, CHIPS, recv=False)
        wait_all(self.back, 1, CHIPS, recv=False)
        self.swap_full.wait_send()


def to_ring(copy_to):
    def go(i, _):
        copy_to(8 + (2 * (i % 2) - 1) * ((i + 1) // 2)).start()
        return 0

    lax.fori_loop(0, DP - 1, go, 0)


class Ring:
    RIGHT, LEFT = 8, 7

    def scratch_gather(parts):
        return [
            pltpu.SemaphoreType.DMA((Ring.RIGHT, parts)),
            pltpu.SemaphoreType.DMA((Ring.RIGHT, parts)),
            pltpu.SemaphoreType.DMA((Ring.LEFT, parts)),
            pltpu.SemaphoreType.DMA((Ring.LEFT, parts)),
        ]

    def all_gather(whole, refs, rows, parts, between=()):
        sr, rr, sl, rl = refs
        dp, _, _, _ = place()
        right, left = {"dp": (dp + 1) % DP}, {"dp": (dp + DP - 1) % DP}
        piece = rows // parts

        def copy_r(s, p):
            part = whole.at[(dp + DP - s) % DP, pl.ds(p * piece, piece)]
            return send(part, part, sr.at[s, p], rr.at[s, p], right)

        def copy_l(s, p):
            part = whole.at[(dp + s) % DP, pl.ds(p * piece, piece)]
            return send(part, part, sl.at[s, p], rl.at[s, p], left)

        for p in range(parts):
            copy_r(0, p).start()
            copy_l(0, p).start()
        if between:
            between[0]()
        for s in range(1, Ring.RIGHT):
            for p in range(parts):
                copy_r(s - 1, p).wait_recv()
                copy_r(s, p).start()
                copy_l(s - 1, p).wait_recv()
                if s < Ring.LEFT:
                    copy_l(s, p).start()
            if s < len(between) and between[s] is not None:
                between[s]()
        for p in range(parts):
            copy_r(Ring.RIGHT - 1, p).wait_recv()

        def finish():
            def drain_r(s, _):
                for p in range(parts):
                    copy_r(s, p).wait_send()
                return 0

            def drain_l(s, _):
                for p in range(parts):
                    copy_l(s, p).wait_send()
                return 0

            lax.fori_loop(0, Ring.RIGHT, drain_r, 0)
            lax.fori_loop(0, Ring.LEFT, drain_l, 0)

        return finish


class FoldedScatter:
    COUNT = 9

    def scratch(rows, width):
        return [
            pltpu.VMEM((4, 3, rows, width), BF16),
            pltpu.VMEM((4, rows, width), BF16),
            pltpu.VMEM((3, rows, width), BF16),
            pltpu.VMEM((rows, width), F32),
            pltpu.SemaphoreType.DMA((4, 3)),
            pltpu.SemaphoreType.DMA((4, 3)),
            pltpu.SemaphoreType.DMA((3,)),
            pltpu.SemaphoreType.DMA((3,)),
            pltpu.VMEM((DP, rows, width), BF16),
        ]

    def __init__(self, local, refs):
        self.local = local
        self.near, self.stage, self.far, self.own, self.ns, self.nr, self.fs, self.fr, self.give = refs
        self.dp = lax.axis_index("dp")
        self.cls, self.row = self.dp % 4, self.dp // 4

    def near_copy(self, o, j):
        q = (self.row + o) % 4
        step = (1, DP - 1, DP - 2 + 4 * (q % 2))[j]
        to = (self.dp + step) % DP
        return send(
            self.give.at[to % 4 + 4 * q], self.near.at[q, j], self.ns.at[q, j], self.nr.at[q, j], {"dp": to}
        )

    def far_copy(self, o):
        q = (self.row + o) % 4
        return send(
            self.stage.at[q], self.far.at[o - 1], self.fs.at[o - 1], self.fr.at[o - 1],
            {"dp": self.cls + 4 * q},
        )

    def start(self):
        self.give[...] = self.local[...].astype(BF16)
        for o in (2, 1, 3, 0):
            for j in range(3):
                self.near_copy(o, j).start()

    def fold(self):
        for o in (2, 1, 3, 0):
            q = (self.row + o) % 4
            total = self.local[self.cls + 4 * q]
            for j in range(3):
                self.near_copy(o, j).wait_recv()
                total = total + self.near[q, j].astype(F32)
            if o:
                self.stage[q] = total.astype(BF16)
                self.far_copy(o).start()
            else:
                self.own[...] = total

    def end(self):
        total = self.own[...]
        for o in (1, 3, 2):
            self.far_copy(o).wait_recv()
            total = total + self.far[o - 1].astype(F32)
        return total

    def drain(self):
        for o in range(4):
            for j in range(3):
                self.near_copy(o, j).wait_send()
            if o:
                self.far_copy(o).wait_send()


def half_rows(h):
    return pl.ds(pl.multiple_of(h * 256, 256), 256)


def dot_t(a, b):
    return lax.dot_general(a, b, (((0,), (0,)), ((), ())), preferred_element_type=F32)


LEAF = 128


def exact_dot(a, b, dims):
    return lax.dot_general(
        a, b, (dims, ((), ())), precision=lax.Precision.HIGHEST, preferred_element_type=F32
    )


def leaf_inverse(block, inverse):
    groups = LEAF // 8
    sub = lax.broadcasted_iota(jnp.int32, (8, 128), 0)

    def spread(row):
        return jnp.broadcast_to(row, (8, 128))

    for p in range(groups):
        cols = {
            g: [spread(block[g][:, 8 * p + j : 8 * p + j + 1]) for j in range(8)]
            for g in range(p, groups)
        }
        pivots = jnp.zeros((8, 128), F32)
        for j in range(8):
            pivot = spread(cols[p][j][j : j + 1, :])
            over = 1.0 / pivot
            pivots = jnp.where(sub == j, pivot, pivots)
            below = jnp.where(sub > j, cols[p][j], 0.0)
            row_block = spread(block[p][j : j + 1, :]) * over
            row_inverse = spread(inverse[p][j : j + 1, :]) * over
            ratio = {i: spread(cols[p][j][i : i + 1, :]) * over for i in range(j + 1, 8)}
            for g in range(p, groups):
                left = below if g == p else cols[g][j]
                for i in range(j + 1, 8):
                    cols[g][i] = cols[g][i] - left * ratio[i]
                block[g] = block[g] - left * row_block
                inverse[g] = inverse[g] - left * row_inverse
        inverse[p] = inverse[p] * lax.rsqrt(pivots)
    return jnp.concatenate(inverse, axis=0)


VMEM = pl.BlockSpec(memory_space=pltpu.VMEM)


N_PLANE = PlaneSum.COUNT
N_FOLD = FoldedScatter.COUNT
N_GATHER = 4
SLICE = 64
WIDE = DP * SLICE


def dp_semaphores():
    return [pltpu.SemaphoreType.DMA((DP - 1,)) for _ in range(2)]


def invert_factor(whole, after_first):
    lane = lax.broadcasted_iota(jnp.int32, (8, 128), 1)
    sub = lax.broadcasted_iota(jnp.int32, (8, 128), 0)
    column = lax.broadcasted_iota(jnp.int32, (LEAF, R), 1)

    def step(k, _):
        here = pl.ds(pl.multiple_of(k * LEAF, LEAF), LEAF)
        corner = whole[here, here]
        block = [corner[8 * g : 8 * g + 8] for g in range(LEAF // 8)]
        unit = [jnp.where(lane == sub + 8 * g, 1.0, 0.0) for g in range(LEAF // 8)]
        inverse = leaf_inverse(block, unit)
        panel = exact_dot(inverse, whole[here, :], ((1,), (0,)))
        below = jnp.where(column >= (k + 1) * LEAF, panel[:, :R], 0.0)
        whole[here, R:] = panel[:, R:]
        whole[...] -= exact_dot(below, panel, ((0,), (0,)))

        @pl.when(k == 0)
        def _():
            after_first()

        return 0

    lax.fori_loop(0, R // LEAF, step, 0)


def galore_kernel(og, tm, act, first, second, update, new_first, new_second, *refs):
    sums = [refs[i * N_PLANE : (i + 1) * N_PLANE] for i in range(3)]
    rest = refs[3 * N_PLANE :]
    fold_refs, rest = rest[:N_FOLD], rest[N_FOLD:]
    gather, rest = rest[:N_GATHER], rest[N_GATHER:]
    sketch_in, local, gram_local, gram, raw, terms, moments, moved, stage, landed, sketch = rest[:11]
    slots, rows_of, factor_work, projected, whole, back, tiles, squares_in = rest[11:19]
    ms, mr, ss, sr, gs, gr, ps, pr, qs, qr, zs, zr, bs, br, slot_pair, sq_pair = rest[19:]
    dp, mp, chip, core = place()
    partner = {"mp": chip * 2 + 1 - core}
    width = og.shape[1]
    barrier, count = greet("all")
    for i in range(DP):
        stop = min(SLICE, width - i * SLICE)
        if stop < SLICE:
            moments[i] = jnp.zeros((32, 2 * SLICE), F32)
        if stop > 0:
            moments[i, :, :stop] = first[:, i * SLICE : i * SLICE + stop]
            moments[i, :, SLICE : SLICE + stop] = second[:, i * SLICE : i * SLICE + stop]
    terms[width // 8 * 8 :, :] = jnp.zeros((WIDE - width // 8 * 8, R), F32)
    factor_work[:, R:] = jnp.where(
        lax.broadcasted_iota(jnp.int32, (R, R), 0) == lax.broadcasted_iota(jnp.int32, (R, R), 1), 1.0, 0.0
    )
    pl.semaphore_wait(barrier, count)

    def in_half(h):
        return jnp.dot(og[half_rows(h), :], tm[...], preferred_element_type=F32)

    sum_in = PlaneSum(in_half, sketch_in, BF16, sums[0])
    sum_in.start()

    def moment_copy(k):
        to = (dp + k) % DP
        return send(moments.at[to], moved.at[dp], ms.at[k - 1], mr.at[k - 1], {"dp": to})

    to_ring(moment_copy)
    moved[dp] = moments[dp]
    sum_in.scatter()
    sum_in.gather()
    sum_in.share()
    near, far = half_rows(core), half_rows(1 - core)
    local[...] = dot_t(act[near, :], sketch_in[near, :]).reshape(DP, 16, R)
    sum_in.end()
    local[...] += dot_t(act[far, :], sketch_in[far, :]).reshape(DP, 16, R)

    stage[...] = local[...].astype(BF16)

    def stage_copy(k):
        to = (dp + k) % DP
        return send(stage.at[to], landed.at[k - 1], ss.at[k - 1], sr.at[k - 1], {"dp": to})

    to_ring(stage_copy)

    def add(k, total):
        stage_copy(k).wait_recv()
        return total + landed[k - 1].astype(F32)

    own = lax.fori_loop(1, DP, add, local[dp]).astype(BF16)
    sketch[dp] = own
    slots[chip, core] = own

    def sketch_copy(k):
        return send(
            sketch.at[dp], sketch.at[dp], gs.at[k - 1], gr.at[k - 1], {"dp": (dp + k) % DP}
        )

    to_ring(sketch_copy)
    slot_gather = plane_gather(slots.at[chip, core], ps, pr)
    slot_half = slots.at[:, core]
    slot_swap = send(slot_half, slot_half, slot_pair.at[0], slot_pair.at[1], partner)
    wait_all(sketch_copy, 1, DP)
    rows_block = sketch[...].reshape(256, R)

    def raw_half(h):
        return jnp.dot(act[half_rows(h), :], rows_block, preferred_element_type=F32)

    def gram_half(h):
        return gram_local[half_rows(h), :]

    sum_raw = PlaneSum(raw_half, raw, BF16, sums[1])
    sum_gram = PlaneSum(gram_half, gram, F32, sums[2])
    sum_raw.start()
    gram_local[...] = dot_t(rows_block, rows_block)
    sum_gram.start()
    sum_raw.scatter()
    sum_gram.scatter()
    sum_raw.gather()
    sum_gram.gather()
    sum_raw.share()
    wait_all(slot_gather, 1, CHIPS)
    slot_swap.start()
    sum_raw.end()

    terms[:width, :] = dot_t(og[...], raw[...])
    fold = FoldedScatter(terms.reshape(DP, SLICE, R), fold_refs)
    fold.start()
    sum_gram.share()
    sum_gram.end()
    factor_work[:, :R] = gram[...]
    invert_factor(factor_work, fold.fold)
    inverse = factor_work[:, R:]
    part = fold.end()
    result = exact_dot(inverse, part, ((1,), (1,)))

    wait_all(moment_copy, 1, DP)
    projected[...] = result.reshape(DP, 32, SLICE)
    both = moved[...].reshape(R, 2 * SLICE)
    new_m = beta_one * both[:, :SLICE] + (1.0 - beta_one) * result
    new_v = beta_two * both[:, SLICE:] + (1.0 - beta_two) * result * result
    correct_one = 1.0 - beta_one**STEP
    correct_two = 1.0 - beta_two**STEP
    direction = new_m / correct_one / (jnp.sqrt(new_v / correct_two) + adam_eps)
    whole[dp] = direction.T.astype(BF16)
    tiles[0] = jnp.broadcast_to(jnp.sum(direction * direction, keepdims=True), (8, 128))
    back[dp] = projected[dp]

    pair_copy = send(tiles.at[0], squares_in.at[0], sq_pair.at[0], sq_pair.at[1], partner)

    def chip_copy(k):
        to = {"mp": chip_at(chip, k) * 2 + core}
        return send(tiles.at[1], squares_in.at[k], qs.at[k - 1], qr.at[k - 1], to)

    def plane_copy(k):
        to = {"dp": (dp + k) % DP}
        return send(tiles.at[2], squares_in.at[15 + k], zs.at[k - 1], zr.at[k - 1], to)

    def back_copy(k):
        to = (dp + k) % DP
        return send(projected.at[to], back.at[dp], bs.at[k - 1], br.at[k - 1], {"dp": to})

    def add_all(copy, base, total):
        def go(k, value):
            copy(k).wait_recv()
            return value + squares_in[base + k]

        return lax.fori_loop(1, 16, go, total)

    def at_start():
        pair_copy.start()
        to_ring(back_copy)
        high = inverse.astype(BF16)
        low = (inverse - high.astype(F32)).astype(BF16)
        slot_swap.wait_recv()
        rows = slots[...].reshape(R, R)
        by_columns = (((1,), (1,)), ((), ()))
        basis = lax.dot_general(rows, high, by_columns, preferred_element_type=F32)
        basis += lax.dot_general(rows, low, by_columns, preferred_element_type=F32)
        rows_of[...] = basis.astype(BF16)

    def after_one():
        pair_copy.wait_recv()
        tiles[1] = tiles[0] + squares_in[0]

        def go(k, _):
            chip_copy(k).start()
            return 0

        lax.fori_loop(1, 16, go, 0)

    def after_three():
        tiles[2] = add_all(chip_copy, 0, tiles[1])
        to_ring(plane_copy)

    def after_five():
        wait_all(back_copy, 1, DP)
        sums_here = jnp.concatenate([back[i] for i in range(DP)], axis=1)[:, :width]
        new_first[...] = beta_one * first[...] + (1.0 - beta_one) * sums_here
        new_second[...] = beta_two * second[...] + (1.0 - beta_two) * sums_here * sums_here

    steps = (at_start, after_one, None, after_three, None, after_five)
    done_gather = Ring.all_gather(whole, gather, SLICE, 2, steps)
    product = lax.dot_general(
        rows_of[...],
        whole[...].reshape(WIDE, R),
        (((1,), (1,)), ((), ())),
        preferred_element_type=F32,
    )
    total_squares = add_all(plane_copy, 15, tiles[2])
    factor = lax.rsqrt(total_squares / (R * FF) + norm_eps)[0:1, 0:1]
    update[...] = (factor * product[:, :width]).astype(BF16)

    for plane in (sum_in, sum_raw, sum_gram):
        plane.drain()
    fold.drain()
    done_gather()
    pair_copy.wait_send()
    slot_swap.wait_send()
    wait_all(slot_gather, 1, CHIPS, recv=False)
    for copy in (stage_copy, sketch_copy, moment_copy, chip_copy, plane_copy, back_copy):
        wait_all(copy, 1, 16, recv=False)


def galore_call(out_grads, test_matrix, activations, first, second):
    return pl.pallas_call(
        galore_kernel,
        out_shape=(
            jax.ShapeDtypeStruct((R, first.shape[1]), BF16),
            jax.ShapeDtypeStruct(first.shape, F32),
            jax.ShapeDtypeStruct(second.shape, F32),
        ),
        in_specs=[VMEM] * 5,
        out_specs=(VMEM,) * 3,
        scratch_shapes=[
            *PlaneSum.scratch(BF16),
            *PlaneSum.scratch(BF16),
            *PlaneSum.scratch(F32),
            *FoldedScatter.scratch(SLICE, R),
            *Ring.scratch_gather(2),
            pltpu.VMEM((R, R), BF16),
            pltpu.VMEM((DP, 16, R), F32),
            pltpu.VMEM((R, R), F32),
            pltpu.VMEM((R, R), F32),
            pltpu.VMEM((R, R), BF16),
            pltpu.VMEM((WIDE, R), F32),
            pltpu.VMEM((DP, 32, 2 * SLICE), F32),
            pltpu.VMEM((DP, 32, 2 * SLICE), F32),
            pltpu.VMEM((DP, 16, R), BF16),
            pltpu.VMEM((DP - 1, 16, R), BF16),
            pltpu.VMEM((DP, 16, R), BF16),
            pltpu.VMEM((CHIPS, 2, 16, R), BF16),
            pltpu.VMEM((R, R), BF16),
            pltpu.VMEM((R, 2 * R), F32),
            pltpu.VMEM((DP, 32, SLICE), F32),
            pltpu.VMEM((DP, SLICE, R), BF16),
            pltpu.VMEM((DP, 32, SLICE), F32),
            pltpu.VMEM((3, 8, 128), F32),
            pltpu.VMEM((31, 8, 128), F32),
            *[sem for _ in range(7) for sem in dp_semaphores()],
            pltpu.SemaphoreType.DMA((2,)),
            pltpu.SemaphoreType.DMA((2,)),
        ],
        compiler_params=pltpu.CompilerParams(
            collective_id=0, has_side_effects=True, vmem_limit_bytes=48 * 2**20
        ),
        name="galore_step",
    )(out_grads, test_matrix, activations, first, second)


def shards(activations, out_grads, test_matrix, first_moment, second_moment):
    update, new_first, new_second = galore_call(
        out_grads, test_matrix, activations, first_moment, second_moment
    )
    return (update.reshape(lax.axis_size("mp"), 16, out_grads.shape[1]), new_first, new_second)


def solution(mesh):
    placed = (P("dp", "mp"), P("dp", "mp"), P("mp", None), P("dp", "mp"), P("dp", "mp"))
    return jax.shard_map(
        shards,
        mesh=mesh,
        in_specs=placed,
        out_specs=(P(None, "dp", "mp"), P("dp", "mp"), P("dp", "mp")),
        check_vma=False,
    )
```

time: 931 us -> 165 us (0.18)
  blocking collectives: 439 us -> 0 us
  waiting for transfers between devices: 311 us -> 0 us
  Pallas kernels: 0 us -> 158 us
  other arithmetic: 122 us -> 0 us
  matrix products: 19.8 us -> 0 us
  local copies, waits for them, and re-layouts: 20.5 us -> 3.89 us
  between operations: 17.3 us -> 0.71 us
    psum x3 -> x0, blocking collectives: 385 us -> none  [the longest x1 135 us: shards(): sketch_in = lax.psum(partial_in, 'mp').astype(jnp.bfloat16)]
    psum x2 -> x0, waiting for transfers between devices: 274 us -> none  [the longest x1 142 us: shards(): gram_matrix = lax.psum(gram_local, 'mp')]
    pallas_call x0 -> x1, Pallas kernels: none -> 158 us  [galore_call(): pl.pallas_call(galore_kernel, out_shape=(jax.ShapeDtypeStruct((R, first.s...]
    another operation x18 -> x0, other arithmetic: 120 us -> none  [the longest x14 78.6 us: orthonormal(): lower_factor = jnp.linalg.cholesky(gram_matrix)]
    all_gather x2 -> x0, blocking collectives: 54.9 us -> none  [the longest x1 27.5 us: shards(): lax.all_gather(direction_b, 'dp', axis=0, tiled=True)]
    reduce_scatter x1 -> x0, waiting for transfers between devices: 37 us -> none  [shards(): lax.psum_scatter(jnp.einsum('tr,tf->rf', columns, out_grads, preferred_el...]
    another operation x17 -> x0, local copies, waits for them, and re-layouts: 14.6 us -> none
    another operation x13 -> x0, matrix products: 10.4 us -> none  [the longest x6 5.47 us: orthonormal(): lower_factor = jnp.linalg.cholesky(gram_matrix)]
  transfers between devices with their start and end apart: 3 -> 0, of which waited for: 3 -> 0; matrix products, arithmetic and copies ran while one was open for 0% -> 0% of each run, Pallas kernels for 0% -> 0%
where the time goes in v3:
time: 165 us; the launch traced here: 162 us
  Pallas kernels  158 us (96%)
  local copies, waits for them, and re-layouts  3.89 us (2%)
    pallas_call x1, Pallas kernels, galore_call(): pl.pallas_call(galore_kernel, out_shape=(jax.ShapeDtypeStruct((R, first.s...  158 us
    unnamed x12, local copies, waits for them, and re-layouts  3.89 us

profile of v3, /device:TPU:1, one launch (start us, length us, event | category | flops | bytes accessed | tf_op | source)
XLA Modules:
  0.0 162.1 jit_solution(12482966147474339974)
XLA Ops:
  0.6 0.0 copy-start.3
  0.6 0.0 copy-start.2
  0.7 0.0 copy-start
  0.7 0.0 copy-start.1
  0.7 1.6 copy.8.og
  2.3 0.0 copy-done.3
  2.3 0.0 copy-done.2
  2.3 0.0 copy-done
  2.3 0.0 copy-done.1
  2.3 157.5 %galore_step.1 = (bf16[512,924]{1,0:T(8,128)(2,1)S(1)}, f32[32,924]{1,0:T(8,128)S(1)}, f32[32,924]{1,0:T(8,128)S(1)}) custom-call(bf16[512,924]{1,0:T(8,128)(2,1)S(1)} %copy.8.og, bf16[924,512]{1,0:T(8,128)(2,1)S(1)} %copy-done, bf16[512,256]{1,0:T(8,128)(2,1)S(1)} %copy-done.1, f32[32,924]{1,0:T(8,128)S(1)} %copy-done.2, f32[32,924]{1,0:T(8,128)S(1)} %copy-done.3), custom_call_target="tpu_custom_call" | custom-call | tf_op jit(solution)/shard_map/galore_step/pallas_call | solution.py:589
  159.8 1.0 copy.12
  160.8 0.7 copy.13
  161.5 0.7 copy.14
Async XLA Ops:
  0.6 1.6 %copy-start.3 = (f32[32,924]{1,0:T(8,128)S(1)}, f32[32,924]{1,0:T(8,128)}, u32[]{:S(2)}) copy-start(f32[32,924]{1,0:T(8,128)} %second.1) | copy-start | bytes 354820
  0.6 1.6 %copy-start.2 = (f32[32,924]{1,0:T(8,128)S(1)}, f32[32,924]{1,0:T(8,128)}, u32[]{:S(2)}) copy-start(f32[32,924]{1,0:T(8,128)} %first.1) | copy-start | bytes 354820
  0.7 1.6 %copy-start = (bf16[924,512]{1,0:T(8,128)(2,1)S(1)}, bf16[924,512]{1,0:T(8,128)(2,1)}, u32[]{:S(2)}) copy-start(bf16[924,512]{1,0:T(8,128)(2,1)} %tm.1) | copy-start | bytes 2838532
  0.7 1.6 %copy-start.1 = (bf16[512,256]{1,0:T(8,128)(2,1)S(1)}, bf16[512,256]{1,0:T(8,128)(2,1)}, u32[]{:S(2)}) copy-start(bf16[512,256]{1,0:T(8,128)(2,1)} %act.1) | copy-start | bytes 786436

commit v4 on v3

v4 whole, which is shorter than its diff:
```python
import jax
import jax.numpy as jnp
from jax import lax
from jax.experimental import pallas as pl
from jax.experimental.pallas import tpu as pltpu
from jax.sharding import PartitionSpec as P

FF = 29568
R = 512
STEP = 100

beta_one = 0.9
beta_two = 0.999
adam_eps = 1e-08
norm_eps = 1e-06

MESH = pl.DeviceIdType.MESH
F32 = jnp.float32
BF16 = jnp.bfloat16
CHIPS = 16
DP = 16


def place():
    mp = lax.axis_index("mp")
    core = mp % 2
    chip = mp // 2
    return lax.axis_index("dp"), mp, chip, core


def chip_at(chip, k):
    x = (chip // 4 + k // 4) % 4
    y = (chip % 4 + k % 4) % 4
    return x * 4 + y


def greet(dp_offsets):
    dp, mp, chip, core = place()
    barrier = pltpu.get_barrier_semaphore()
    pl.semaphore_signal(barrier, inc=1, device_id={"mp": chip * 2 + 1 - core}, device_id_type=MESH)

    def to_chip(k, _):
        pl.semaphore_signal(
            barrier, inc=1, device_id={"mp": chip_at(chip, k) * 2 + core}, device_id_type=MESH
        )
        return 0

    lax.fori_loop(1, CHIPS, to_chip, 0)

    def to_ring(k, _):
        pl.semaphore_signal(barrier, inc=1, device_id={"dp": (dp + k) % DP}, device_id_type=MESH)
        return 0

    if dp_offsets == "all":
        lax.fori_loop(1, DP, to_ring, 0)
        return barrier, 1 + (CHIPS - 1) + (DP - 1)
    to_ring(1, 0)
    to_ring(DP - 1, 0)
    return barrier, 1 + (CHIPS - 1) + 2


def send(src, dst, sends, recvs, where):
    return pltpu.make_async_remote_copy(
        src_ref=src, dst_ref=dst, send_sem=sends, recv_sem=recvs, device_id=where, device_id_type=MESH
    )


def plane_scatter(stage, landed, sends, recvs):
    _, _, chip, core = place()

    def copy(k):
        there = chip_at(chip, k)
        return send(
            stage.at[there], landed.at[k - 1], sends.at[k - 1], recvs.at[k - 1], {"mp": there * 2 + core}
        )

    def go(k, _):
        copy(k).start()
        return 0

    lax.fori_loop(1, CHIPS, go, 0)
    return copy


def plane_gather(block, sends, recvs):
    _, _, chip, core = place()

    def copy(k):
        there = chip_at(chip, k)
        return send(block, block, sends.at[k - 1], recvs.at[k - 1], {"mp": there * 2 + core})

    def go(k, _):
        copy(k).start()
        return 0

    lax.fori_loop(1, CHIPS, go, 0)
    return copy


def wait_all(copy, first, last, recv=True):
    def step(k, _):
        if recv:
            copy(k).wait_recv()
        else:
            copy(k).wait_send()
        return 0

    lax.fori_loop(first, last, step, 0)


class PlaneSum:
    COUNT = 9

    def scratch(kind, half=256, width=R):
        return [
            pltpu.VMEM((half, width), kind),
            pltpu.VMEM((half, width), kind),
            pltpu.VMEM((CHIPS, half // CHIPS, width), kind),
            pltpu.VMEM((CHIPS - 1, half // CHIPS, width), kind),
            pltpu.SemaphoreType.DMA((4,)),
            pltpu.SemaphoreType.DMA((CHIPS - 1,)),
            pltpu.SemaphoreType.DMA((CHIPS - 1,)),
            pltpu.SemaphoreType.DMA((CHIPS - 1,)),
            pltpu.SemaphoreType.DMA((CHIPS - 1,)),
        ]

    def __init__(self, half_of, full, kind, refs):
        self.half_of, self.full, self.kind = half_of, full, kind
        self.give, self.take, self.stage, self.landed, pair, self.s1, self.r1, self.s2, self.r2 = refs
        _, _, self.chip, self.core = place()
        partner = {"mp": self.chip * 2 + 1 - self.core}
        self.swap = send(self.give, self.take, pair.at[0], pair.at[1], partner)
        self.rows = full.shape[0] // 2
        half = full.at[half_rows(self.core, self.rows), :]
        self.swap_full = send(half, half, pair.at[2], pair.at[3], partner)

    def fill(self):
        self.give[...] = self.half_of(1 - self.core).astype(self.kind)

    def start(self):
        self.fill()
        self.swap.start()

    def scatter(self):
        own = self.half_of(self.core)
        self.swap.wait_recv()
        both = own + self.take[...].astype(F32)
        self.stage[...] = both.astype(self.kind).reshape(self.stage.shape)
        self.out = plane_scatter(self.stage, self.landed, self.s1, self.r1)

    def gather(self):
        def add(k, total):
            self.out(k).wait_recv()
            return total + self.landed[k - 1].astype(F32)

        total = lax.fori_loop(1, CHIPS, add, self.stage[self.chip].astype(F32))
        count = self.rows // CHIPS
        mine = pl.ds(pl.multiple_of(self.core * self.rows + self.chip * count, count), count)
        self.full[mine, :] = total.astype(self.kind)
        self.back = plane_gather(self.full.at[mine, :], self.s2, self.r2)

    def share(self):
        wait_all(self.back, 1, CHIPS)
        self.swap_full.start()

    def end(self):
        self.swap_full.wait_recv()

    def drain(self):
        self.swap.wait_send()
        wait_all(self.out, 1, CHIPS, recv=False)
        wait_all(self.back, 1, CHIPS, recv=False)
        self.swap_full.wait_send()


def to_ring(copy_to):
    def go(i, _):
        copy_to(8 + (2 * (i % 2) - 1) * ((i + 1) // 2)).start()
        return 0

    lax.fori_loop(0, DP - 1, go, 0)


class FoldedScatter:
    COUNT = 9

    def scratch(rows, width):
        return [
            pltpu.VMEM((4, 3, rows, width), BF16),
            pltpu.VMEM((4, rows, width), BF16),
            pltpu.VMEM((3, rows, width), BF16),
            pltpu.VMEM((rows, width), F32),
            pltpu.SemaphoreType.DMA((4, 3)),
            pltpu.SemaphoreType.DMA((4, 3)),
            pltpu.SemaphoreType.DMA((3,)),
            pltpu.SemaphoreType.DMA((3,)),
            pltpu.VMEM((DP, rows, width), BF16),
        ]

    def __init__(self, local, refs):
        self.local = local
        self.near, self.stage, self.far, self.own, self.ns, self.nr, self.fs, self.fr, self.give = refs
        self.dp = lax.axis_index("dp")
        self.cls, self.row = self.dp % 4, self.dp // 4

    def near_copy(self, o, j):
        q = (self.row + o) % 4
        step = (1, DP - 1, DP - 2 + 4 * (q % 2))[j]
        to = (self.dp + step) % DP
        return send(
            self.give.at[to % 4 + 4 * q], self.near.at[q, j], self.ns.at[q, j], self.nr.at[q, j], {"dp": to}
        )

    def far_copy(self, o):
        q = (self.row + o) % 4
        return send(
            self.stage.at[q], self.far.at[o - 1], self.fs.at[o - 1], self.fr.at[o - 1],
            {"dp": self.cls + 4 * q},
        )

    def start(self):
        for b in range(DP):
            self.give[b] = self.local(b).astype(BF16)
        for o in (2, 1, 3, 0):
            for j in range(3):
                self.near_copy(o, j).start()

    def fold(self):
        for o in (2, 1, 3, 0):
            q = (self.row + o) % 4
            total = self.local(self.cls + 4 * q)
            for j in range(3):
                self.near_copy(o, j).wait_recv()
                total = total + self.near[q, j].astype(F32)
            if o:
                self.stage[q] = total.astype(BF16)
                self.far_copy(o).start()
            else:
                self.own[...] = total

    def end(self):
        total = self.own[...]
        for o in (1, 3, 2):
            self.far_copy(o).wait_recv()
            total = total + self.far[o - 1].astype(F32)
        return total

    def drain(self):
        for o in range(4):
            for j in range(3):
                self.near_copy(o, j).wait_send()
            if o:
                self.far_copy(o).wait_send()


class FoldedGather:
    COUNT = 4

    def scratch():
        return [
            pltpu.SemaphoreType.DMA((3,)),
            pltpu.SemaphoreType.DMA((3,)),
            pltpu.SemaphoreType.DMA((4, 3)),
            pltpu.SemaphoreType.DMA((4, 3)),
        ]

    def __init__(self, whole, refs):
        self.whole = whole
        self.fs, self.fr, self.ns, self.nr = refs
        self.dp = lax.axis_index("dp")
        self.cls, self.row = self.dp % 4, self.dp // 4

    def far_copy(self, o):
        own = self.whole.at[self.dp]
        to = self.cls + 4 * ((self.row + o) % 4)
        return send(own, own, self.fs.at[o - 1], self.fr.at[o - 1], {"dp": to})

    def near_copy(self, q, j):
        block = self.whole.at[self.cls + 4 * q]
        step = (1, DP - 1, 2 + (DP - 4) * (q % 2))[j]
        return send(
            block, block, self.ns.at[q, j], self.nr.at[q, j], {"dp": (self.dp + step) % DP}
        )

    def start(self):
        for o in (2, 1, 3):
            self.far_copy(o).start()
        for j in range(3):
            self.near_copy(self.row, j).start()

    def forward(self):
        for o in (1, 3, 2):
            self.far_copy(o).wait_recv()
            for j in range(3):
                self.near_copy((self.row + 4 - o) % 4, j).start()

    def end(self):
        for q in range(4):
            for j in range(3):
                self.near_copy(q, j).wait_recv()

    def drain(self):
        for o in range(1, 4):
            self.far_copy(o).wait_send()
        for q in range(4):
            for j in range(3):
                self.near_copy(q, j).wait_send()


def half_rows(h, count=256):
    return pl.ds(pl.multiple_of(h * count, count), count)


def dot_t(a, b):
    return lax.dot_general(a, b, (((0,), (0,)), ((), ())), preferred_element_type=F32)


LEAF = 128


def exact_dot(a, b, dims):
    return lax.dot_general(
        a, b, (dims, ((), ())), precision=lax.Precision.HIGHEST, preferred_element_type=F32
    )


def leaf_inverse(block, inverse):
    groups = LEAF // 8
    sub = lax.broadcasted_iota(jnp.int32, (8, 128), 0)

    def spread(row):
        return jnp.broadcast_to(row, (8, 128))

    for p in range(groups):
        cols = {
            g: [spread(block[g][:, 8 * p + j : 8 * p + j + 1]) for j in range(8)]
            for g in range(p, groups)
        }
        pivots = jnp.zeros((8, 128), F32)
        for j in range(8):
            pivot = spread(cols[p][j][j : j + 1, :])
            over = 1.0 / pivot
            pivots = jnp.where(sub == j, pivot, pivots)
            below = jnp.where(sub > j, cols[p][j], 0.0)
            row_block = spread(block[p][j : j + 1, :]) * over
            row_inverse = spread(inverse[p][j : j + 1, :]) * over
            ratio = {i: spread(cols[p][j][i : i + 1, :]) * over for i in range(j + 1, 8)}
            for g in range(p, groups):
                left = below if g == p else cols[g][j]
                for i in range(j + 1, 8):
                    cols[g][i] = cols[g][i] - left * ratio[i]
                block[g] = block[g] - left * row_block
                inverse[g] = inverse[g] - left * row_inverse
        inverse[p] = inverse[p] * lax.rsqrt(pivots)
    return jnp.concatenate(inverse, axis=0)


VMEM = pl.BlockSpec(memory_space=pltpu.VMEM)


N_PLANE = PlaneSum.COUNT
N_FOLD = FoldedScatter.COUNT
N_GATHER = FoldedGather.COUNT
SLICE = 64
WIDE = DP * SLICE
HALF = R // 2
LEAVES = R // LEAF
UPPER = [(i, j) for i in range(LEAVES) for j in range(i, LEAVES)]
PACKED = len(UPPER) * LEAF


def dp_semaphores():
    return [pltpu.SemaphoreType.DMA((DP - 1,)) for _ in range(2)]


def eliminate(work, k):
    lane = lax.broadcasted_iota(jnp.int32, (8, 128), 1)
    sub = lax.broadcasted_iota(jnp.int32, (8, 128), 0)
    here, after = k * LEAF, (k + 1) * LEAF
    tail = R - after
    block = [work[here + 8 * g : here + 8 * g + 8, here:after] for g in range(LEAF // 8)]
    unit = [jnp.where(lane == sub + 8 * g, 1.0, 0.0) for g in range(LEAF // 8)]
    inverse = leaf_inverse(block, unit)
    panel = exact_dot(inverse, work[here:after, after : R + here], ((1,), (0,)))
    panel = jnp.concatenate([panel, inverse], axis=1)
    work[here:after, R : R + after] = panel[:, tail:]
    if tail:
        work[after:, after : R + after] -= exact_dot(panel[:, :tail], panel, ((0,), (0,)))


def galore_kernel(ogt_in, tm_in, act_in, first_in, second_in, update, sums_out, *refs):
    sums = [refs[i * N_PLANE : (i + 1) * N_PLANE] for i in range(3)]
    rest = refs[3 * N_PLANE :]
    fold_refs, rest = (rest[:N_FOLD], rest[N_FOLD : 2 * N_FOLD]), rest[2 * N_FOLD :]
    gather_refs, rest = (rest[:N_GATHER], rest[N_GATHER : 2 * N_GATHER]), rest[2 * N_GATHER :]
    sketch_in, local, gram_local, gram, raw, terms, moments, moved, stage, landed, sketch = rest[:11]
    slots, rows_of, work, projected, whole_one, whole_two, back, tiles, squares_in = rest[11:20]
    ms, mr, ss, sr, gs, gr, ps, pr, qs, qr, zs, zr, bs, br, slot_pair, sq_pair = rest[20:36]
    ogt, tm, act, first, second, load_sems = rest[36:]
    dp, mp, chip, core = place()
    partner = {"mp": chip * 2 + 1 - core}
    width = ogt.shape[0]
    pairs = ((ogt_in, ogt), (tm_in, tm), (act_in, act), (first_in, first), (second_in, second))
    loads = [pltpu.make_async_copy(a, b, load_sems.at[i]) for i, (a, b) in enumerate(pairs)]
    for load in loads:
        load.start()
    barrier, count = greet("all")
    loads[0].wait()
    loads[1].wait()

    def in_half(h):
        return dot_t(ogt[:, half_rows(h)], tm[...])

    sum_in = PlaneSum(in_half, sketch_in, BF16, sums[0])
    sum_in.fill()
    pl.semaphore_wait(barrier, count)
    sum_in.swap.start()

    def moment_copy(k):
        to = (dp + k) % DP
        return send(moments.at[to], moved.at[dp], ms.at[k - 1], mr.at[k - 1], {"dp": to})

    sum_in.scatter()
    loads[3].wait()
    loads[4].wait()
    for i in range(DP):
        stop = min(SLICE, width - i * SLICE)
        if stop < SLICE:
            moments[i] = jnp.zeros((32, 2 * SLICE), F32)
        if stop > 0:
            moments[i, :, :stop] = first[:, i * SLICE : i * SLICE + stop]
            moments[i, :, SLICE : SLICE + stop] = second[:, i * SLICE : i * SLICE + stop]
    to_ring(moment_copy)
    moved[dp] = moments[dp]
    sum_in.gather()
    terms[width // 8 * 8 :, :] = jnp.zeros((WIDE - width // 8 * 8, R), F32)
    work[:, R:] = jnp.zeros((R, R), F32)
    sum_in.share()
    loads[2].wait()
    near, far = half_rows(core), half_rows(1 - core)
    local[...] = dot_t(act[near, :], sketch_in[near, :]).reshape(DP, 16, R)
    sum_in.end()
    local[...] += dot_t(act[far, :], sketch_in[far, :]).reshape(DP, 16, R)

    stage[...] = local[...].astype(BF16)

    def stage_copy(k):
        to = (dp + k) % DP
        return send(stage.at[to], landed.at[k - 1], ss.at[k - 1], sr.at[k - 1], {"dp": to})

    to_ring(stage_copy)

    def add(k, total):
        stage_copy(k).wait_recv()
        return total + landed[k - 1].astype(F32)

    own = lax.fori_loop(1, DP, add, local[dp]).astype(BF16)
    sketch[dp] = own
    slots[chip, core] = own

    def sketch_copy(k):
        return send(
            sketch.at[dp], sketch.at[dp], gs.at[k - 1], gr.at[k - 1], {"dp": (dp + k) % DP}
        )

    to_ring(sketch_copy)
    slot_gather = plane_gather(slots.at[chip, core], ps, pr)
    slot_half = slots.at[:, core]
    slot_swap = send(slot_half, slot_half, slot_pair.at[0], slot_pair.at[1], partner)
    wait_all(sketch_copy, 1, DP)
    rows_block = sketch[...].reshape(256, R)

    def raw_half(h):
        return jnp.dot(act[half_rows(h), :], rows_block, preferred_element_type=F32)

    def gram_half(h):
        return gram_local[half_rows(h, PACKED // 2), :]

    sum_raw = PlaneSum(raw_half, raw, BF16, sums[1])
    sum_gram = PlaneSum(gram_half, gram, F32, sums[2])
    sum_raw.start()
    for i in range(LEAVES):
        row = dot_t(rows_block[:, i * LEAF : (i + 1) * LEAF], rows_block[:, i * LEAF :])
        for j in range(i, LEAVES):
            at = UPPER.index((i, j)) * LEAF
            gram_local[at : at + LEAF, :] = row[:, (j - i) * LEAF : (j - i + 1) * LEAF]
    sum_gram.start()
    sum_raw.scatter()
    sum_gram.scatter()
    sum_raw.gather()
    sum_gram.gather()
    sum_raw.share()
    wait_all(slot_gather, 1, CHIPS)
    slot_swap.start()
    sum_raw.end()

    terms[:width, :] = jnp.dot(ogt[...], raw[...], preferred_element_type=F32)

    def terms_of(columns):
        def block(b):
            if isinstance(b, int):
                return terms[b * SLICE : (b + 1) * SLICE, columns]
            return terms[pl.ds(pl.multiple_of(b * SLICE, SLICE), SLICE), columns]

        return block

    fold_one = FoldedScatter(terms_of(slice(0, HALF)), fold_refs[0])
    fold_two = FoldedScatter(terms_of(slice(HALF, R)), fold_refs[1])
    fold_one.start()
    sum_gram.share()
    fold_two.start()
    sum_gram.end()
    for n, (i, j) in enumerate(UPPER):
        work[i * LEAF : (i + 1) * LEAF, j * LEAF : (j + 1) * LEAF] = gram[n * LEAF : (n + 1) * LEAF, :]

    def adam(h, result, whole):
        by_owner = result.reshape(8, 2, 16, SLICE)
        projected[8 * h : 8 * h + 8] = jnp.concatenate([by_owner[:, 0], by_owner[:, 1]], axis=2)
        both = moved[8 * h : 8 * h + 8].reshape(HALF, 2 * SLICE)
        new_m = beta_one * both[:, :SLICE] + (1.0 - beta_one) * result
        new_v = beta_two * both[:, SLICE:] + (1.0 - beta_two) * result * result
        correct_one = 1.0 - beta_one**STEP
        correct_two = 1.0 - beta_two**STEP
        direction = new_m / correct_one / (jnp.sqrt(new_v / correct_two) + adam_eps)
        whole[dp] = direction.T.astype(BF16)
        return jnp.sum(direction * direction, keepdims=True)

    gather_one = FoldedGather(whole_one, gather_refs[0])
    gather_two = FoldedGather(whole_two, gather_refs[1])
    by_columns = (((1,), (1,)), ((), ()))

    def basis_columns(k):
        here, after = k * LEAF, (k + 1) * LEAF
        inverse = work[here:after, R : R + after]
        high = inverse.astype(BF16)
        low = (inverse - high.astype(F32)).astype(BF16)
        rows = slots[...].reshape(R, R)[:, :after]
        columns = lax.dot_general(rows, high, by_columns, preferred_element_type=F32)
        columns += lax.dot_general(rows, low, by_columns, preferred_element_type=F32)
        rows_of[:, here:after] = columns.astype(BF16)

    def ring_copy(k):
        to = {"dp": (dp + k) % DP}
        return send(tiles.at[0], squares_in.at[15 + k], zs.at[k - 1], zr.at[k - 1], to)

    pair_copy = send(tiles.at[1], squares_in.at[0], sq_pair.at[0], sq_pair.at[1], partner)

    def chip_copy(k):
        to = {"mp": chip_at(chip, k) * 2 + core}
        return send(tiles.at[2], squares_in.at[k], qs.at[k - 1], qr.at[k - 1], to)

    def back_copy(k):
        to = (dp + k) % DP
        return send(projected.at[to], back.at[dp], bs.at[k - 1], br.at[k - 1], {"dp": to})

    def back_start(h):
        def go(k, _):
            @pl.when((dp + k) % DP // (DP // 2) == h)
            def _():
                back_copy(k).start()

            return 0

        lax.fori_loop(1, DP, go, 0)

    def add_all(copy, base, total):
        def go(k, value):
            copy(k).wait_recv()
            return value + squares_in[base + k]

        return lax.fori_loop(1, 16, go, total)

    eliminate(work, 0)
    fold_one.fold()
    eliminate(work, 1)
    fold_two.fold()
    eliminate(work, 2)
    slot_swap.wait_recv()
    for k in range(LEAVES - 1):
        basis_columns(k)
    for plane in (sum_in, sum_raw, sum_gram):
        plane.drain()
    slot_swap.wait_send()
    wait_all(slot_gather, 1, CHIPS, recv=False)
    for copy in (stage_copy, sketch_copy, moment_copy):
        wait_all(copy, 1, DP, recv=False)
    wait_all(moment_copy, 1, DP)
    part_one = fold_one.end()
    squares = adam(0, exact_dot(work[:HALF, R : R + HALF], part_one, ((1,), (1,))), whole_one)
    gather_one.start()
    back_start(0)
    eliminate(work, LEAVES - 1)
    basis_columns(LEAVES - 1)
    result = exact_dot(work[HALF:, R : R + HALF], part_one, ((1,), (1,)))
    part_two = fold_two.end()
    result += exact_dot(work[HALF:, R + HALF :], part_two, ((1,), (1,)))
    squares += adam(1, result, whole_two)
    tiles[0] = jnp.broadcast_to(squares, (8, 128))
    to_ring(ring_copy)
    gather_two.start()
    back_start(1)
    back[dp] = projected[dp]
    gather_one.forward()
    fold_one.drain()
    fold_two.drain()
    tiles[1] = add_all(ring_copy, 15, tiles[0])
    pair_copy.start()
    gather_two.forward()
    pair_copy.wait_recv()
    tiles[2] = tiles[1] + squares_in[0]

    def chip_start(k, _):
        chip_copy(k).start()
        return 0

    lax.fori_loop(1, CHIPS, chip_start, 0)
    gather_one.end()

    def product_of(columns, whole):
        return lax.dot_general(
            rows_of[:, columns],
            whole[...].reshape(WIDE, HALF),
            by_columns,
            preferred_element_type=F32,
        )

    product = product_of(slice(0, HALF), whole_one)
    wait_all(back_copy, 1, DP)
    for r in range(2):
        rows = [back[i, :, r * SLICE : (r + 1) * SLICE] for i in range(DP)]
        sums_out[16 * r : 16 * r + 16, :] = jnp.concatenate(rows, axis=1)[:, :width]
    total_squares = add_all(chip_copy, 0, tiles[2])
    factor = lax.rsqrt(total_squares / (R * FF) + norm_eps)[0:1, 0:1]
    for copy in (ring_copy, back_copy, chip_copy):
        wait_all(copy, 1, 16, recv=False)
    pair_copy.wait_send()
    gather_one.drain()
    gather_two.end()
    product += product_of(slice(HALF, R), whole_two)
    update[...] = (factor * product[:, :width]).astype(BF16)
    gather_two.drain()


def galore_call(out_grads, test_matrix, activations, first, second):
    return pl.pallas_call(
        galore_kernel,
        out_shape=(
            jax.ShapeDtypeStruct((R, first.shape[1]), BF16),
            jax.ShapeDtypeStruct(first.shape, F32),
        ),
        in_specs=[pl.BlockSpec(memory_space=pltpu.HBM)] * 5,
        out_specs=(VMEM,) * 2,
        scratch_shapes=[
            *PlaneSum.scratch(BF16),
            *PlaneSum.scratch(BF16),
            *PlaneSum.scratch(F32, PACKED // 2, LEAF),
            *FoldedScatter.scratch(SLICE, HALF),
            *FoldedScatter.scratch(SLICE, HALF),
            *FoldedGather.scratch(),
            *FoldedGather.scratch(),
            pltpu.VMEM((R, R), BF16),
            pltpu.VMEM((DP, 16, R), F32),
            pltpu.VMEM((PACKED, LEAF), F32),
            pltpu.VMEM((PACKED, LEAF), F32),
            pltpu.VMEM((R, R), BF16),
            pltpu.VMEM((WIDE, R), F32),
            pltpu.VMEM((DP, 32, 2 * SLICE), F32),
            pltpu.VMEM((DP, 32, 2 * SLICE), F32),
            pltpu.VMEM((DP, 16, R), BF16),
            pltpu.VMEM((DP - 1, 16, R), BF16),
            pltpu.VMEM((DP, 16, R), BF16),
            pltpu.VMEM((CHIPS, 2, 16, R), BF16),
            pltpu.VMEM((R, R), BF16),
            pltpu.VMEM((R, 2 * R), F32),
            pltpu.VMEM((DP, 16, 2 * SLICE), F32),
            pltpu.VMEM((DP, SLICE, HALF), BF16),
            pltpu.VMEM((DP, SLICE, HALF), BF16),
            pltpu.VMEM((DP, 16, 2 * SLICE), F32),
            pltpu.VMEM((3, 8, 128), F32),
            pltpu.VMEM((31, 8, 128), F32),
            *[sem for _ in range(7) for sem in dp_semaphores()],
            pltpu.SemaphoreType.DMA((2,)),
            pltpu.SemaphoreType.DMA((2,)),
            pltpu.VMEM(out_grads.shape[::-1], BF16),
            pltpu.VMEM(test_matrix.shape, BF16),
            pltpu.VMEM(activations.shape, BF16),
            pltpu.VMEM(first.shape, F32),
            pltpu.VMEM(second.shape, F32),
            pltpu.SemaphoreType.DMA((5,)),
        ],
        compiler_params=pltpu.CompilerParams(
            collective_id=0, has_side_effects=True, vmem_limit_bytes=60 * 2**20
        ),
        name="galore_step",
    )(out_grads.T, test_matrix, activations, first, second)


def shards(activations, out_grads, test_matrix, first_moment, second_moment):
    update, projected = galore_call(
        out_grads, test_matrix, activations, first_moment, second_moment
    )
    new_first = beta_one * first_moment + (1.0 - beta_one) * projected
    new_second = beta_two * second_moment + (1.0 - beta_two) * projected * projected
    return (update.reshape(lax.axis_size("mp"), 16, out_grads.shape[1]), new_first, new_second)


def solution(mesh):
    placed = (P("dp", "mp"), P("dp", "mp"), P("mp", None), P("dp", "mp"), P("dp", "mp"))
    return jax.shard_map(
        shards,
        mesh=mesh,
        in_specs=placed,
        out_specs=(P(None, "dp", "mp"), P("dp", "mp"), P("dp", "mp")),
        check_vma=False,
    )
```

time: 165 us -> 148 us (0.90); the launches traced: 162 us -> 148 us
  Pallas kernels: 158 us -> 143 us
    pallas_call x1, Pallas kernels: 158 us -> 143 us  [galore_call(): pl.pallas_call(galore_kernel, out_shape=(jax.ShapeDtypeStruct((R, first.s...]
    unnamed x12 -> x5, local copies, waits for them, and re-layouts: 3.89 us -> 2.31 us
where the time goes in v4:
time: 148 us
  Pallas kernels  143 us (97%)
  local copies, waits for them, and re-layouts  2.31 us (2%)
  other arithmetic  1.64 us (1%)
    pallas_call x1, Pallas kernels, galore_call(): pl.pallas_call(galore_kernel, out_shape=(jax.ShapeDtypeStruct((R, first.s...  143 us

profile of v4, /device:TPU:1, one launch (start us, length us, event | category | flops | bytes accessed | tf_op | source)
XLA Modules:
  0.0 148.1 jit_solution(5078407774239611546)
XLA Ops:
  0.6 0.0 copy-start
  0.6 0.0 copy-start.1
  0.7 143.5 %galore_step.1 = (bf16[512,924]{1,0:T(8,128)(2,1)}, f32[32,924]{1,0:T(8,128)}) custom-call(bf16[924,512]{1,0:T(8,128)(2,1)} %bitcast.3, bf16[924,512]{1,0:T(8,128)(2,1)} %tm_in.1, bf16[512,256]{1,0:T(8,128)(2,1)} %act_in.1, f32[32,924]{1,0:T(8,128)} %first_in.1, f32[32,924]{1,0:T(8,128)} %second_in.1), custom_call_target="tpu_custom_call" | custom-call | tf_op jit(solution)/shard_map/galore_step/pallas_call | solution.py:645
  144.1 0.0 copy-done
  144.1 0.0 copy-done.1
  144.1 1.6 %fusion = (f32[32,924]{1,0:T(8,128)}, f32[32,924]{1,0:T(8,128)}) fusion(f32[32,924]{1,0:T(8,128)} %get-tuple-element.6, f32[32,924]{1,0:T(8,128)S(1)} %copy-done.1, f32[32,924]{1,0:T(8,128)S(1)} %copy-done), kind=kLoop, calls=%fused_computation.1 | loop fusion | flops 206976 | bytes 591360 | tf_op jit(solution)/shard_map/add | solution.py:703
  145.8 2.3 %copy.9 = bf16[32,16,924]{2,1,0:T(8,128)(2,1)} copy(bf16[32,16,924]{2,1,0:T(8,128)(2,1)} %bitcast.2) | data formatting | bytes 1892352
Async XLA Ops:
  0.6 143.5 %copy-start = (f32[32,924]{1,0:T(8,128)S(1)}, f32[32,924]{1,0:T(8,128)}, u32[]{:S(2)}) copy-start(f32[32,924]{1,0:T(8,128)} %first_in.1) | copy-start | bytes 354820
  0.6 143.5 %copy-start.1 = (f32[32,924]{1,0:T(8,128)S(1)}, f32[32,924]{1,0:T(8,128)}, u32[]{:S(2)}) copy-start(f32[32,924]{1,0:T(8,128)} %second_in.1) | copy-start | bytes 354820

commit v5 on v4

--- a/solution.py
+++ b/solution.py
@@ -363,7 +363,8 @@
 N_GATHER = FoldedGather.COUNT
 SLICE = 64
 WIDE = DP * SLICE
-HALF = R // 2
+FIRST = 3 * R // 4
+AHEAD = FIRST // 32
 LEAVES = R // LEAF
 UPPER = [(i, j) for i in range(LEAVES) for j in range(i, LEAVES)]
 PACKED = len(UPPER) * LEAF
@@ -413,24 +414,24 @@
 
     sum_in = PlaneSum(in_half, sketch_in, BF16, sums[0])
     sum_in.fill()
-    pl.semaphore_wait(barrier, count)
-    sum_in.swap.start()
-
-    def moment_copy(k):
-        to = (dp + k) % DP
-        return send(moments.at[to], moved.at[dp], ms.at[k - 1], mr.at[k - 1], {"dp": to})
-
-    sum_in.scatter()
     loads[3].wait()
     loads[4].wait()
     for i in range(DP):
         stop = min(SLICE, width - i * SLICE)
         if stop < SLICE:
-            moments[i] = jnp.zeros((32, 2 * SLICE), F32)
+            moments[i] = jnp.zeros((32, 2 * SLICE), BF16)
         if stop > 0:
-            moments[i, :, :stop] = first[:, i * SLICE : i * SLICE + stop]
-            moments[i, :, SLICE : SLICE + stop] = second[:, i * SLICE : i * SLICE + stop]
+            moments[i, :, :stop] = first[:, i * SLICE : i * SLICE + stop].astype(BF16)
+            moments[i, :, SLICE : SLICE + stop] = second[:, i * SLICE : i * SLICE + stop].astype(BF16)
+    pl.semaphore_wait(barrier, count)
+    sum_in.swap.start()
+
+    def moment_copy(k):
+        to = (dp + k) % DP
+        return send(moments.at[to], moved.at[dp], ms.at[k - 1], mr.at[k - 1], {"dp": to})
+
     to_ring(moment_copy)
+    sum_in.scatter()
     moved[dp] = moments[dp]
     sum_in.gather()
     terms[width // 8 * 8 :, :] = jnp.zeros((WIDE - width // 8 * 8, R), F32)
@@ -504,8 +505,8 @@
 
         return block
 
-    fold_one = FoldedScatter(terms_of(slice(0, HALF)), fold_refs[0])
-    fold_two = FoldedScatter(terms_of(slice(HALF, R)), fold_refs[1])
+    fold_one = FoldedScatter(terms_of(slice(0, FIRST)), fold_refs[0])
+    fold_two = FoldedScatter(terms_of(slice(FIRST, R)), fold_refs[1])
     fold_one.start()
     sum_gram.share()
     fold_two.start()
@@ -513,10 +514,12 @@
     for n, (i, j) in enumerate(UPPER):
         work[i * LEAF : (i + 1) * LEAF, j * LEAF : (j + 1) * LEAF] = gram[n * LEAF : (n + 1) * LEAF, :]
 
-    def adam(h, result, whole):
-        by_owner = result.reshape(8, 2, 16, SLICE)
-        projected[8 * h : 8 * h + 8] = jnp.concatenate([by_owner[:, 0], by_owner[:, 1]], axis=2)
-        both = moved[8 * h : 8 * h + 8].reshape(HALF, 2 * SLICE)
+    def adam(owners, result, whole):
+        count = owners.stop - owners.start
+        by_owner = result.reshape(count, 2, 16, SLICE)
+        packed = jnp.concatenate([by_owner[:, 0], by_owner[:, 1]], axis=2)
+        projected[owners] = packed.astype(BF16)
+        both = moved[owners].astype(F32).reshape(count * 32, 2 * SLICE)
         new_m = beta_one * both[:, :SLICE] + (1.0 - beta_one) * result
         new_v = beta_two * both[:, SLICE:] + (1.0 - beta_two) * result * result
         correct_one = 1.0 - beta_one**STEP
@@ -555,7 +558,7 @@
 
     def back_start(h):
         def go(k, _):
-            @pl.when((dp + k) % DP // (DP // 2) == h)
+            @pl.when((dp + k) % DP // AHEAD == h)
             def _():
                 back_copy(k).start()
 
@@ -586,16 +589,17 @@
         wait_all(copy, 1, DP, recv=False)
     wait_all(moment_copy, 1, DP)
     part_one = fold_one.end()
-    squares = adam(0, exact_dot(work[:HALF, R : R + HALF], part_one, ((1,), (1,))), whole_one)
+    result = exact_dot(work[:FIRST, R : R + FIRST], part_one, ((1,), (1,)))
+    squares = adam(slice(0, AHEAD), result, whole_one)
     gather_one.start()
     back_start(0)
     eliminate(work, LEAVES - 1)
     basis_columns(LEAVES - 1)
-    result = exact_dot(work[HALF:, R : R + HALF], part_one, ((1,), (1,)))
+    result = exact_dot(work[FIRST:, R : R + FIRST], part_one, ((1,), (1,)))
     part_two = fold_two.end()
-    result += exact_dot(work[HALF:, R + HALF :], part_two, ((1,), (1,)))
-    squares += adam(1, result, whole_two)
-    tiles[0] = jnp.broadcast_to(squares, (8, 128))
+    result += exact_dot(work[FIRST:, R + FIRST :], part_two, ((1,), (1,)))
+    squares += adam(slice(AHEAD, DP), result, whole_two)
+    tiles[0] = jnp.broadcast_to(squares, (1, 128))
     to_ring(ring_copy)
     gather_two.start()
     back_start(1)
@@ -619,15 +623,15 @@
     def product_of(columns, whole):
         return lax.dot_general(
             rows_of[:, columns],
-            whole[...].reshape(WIDE, HALF),
+            whole[...].reshape(WIDE, whole.shape[2]),
             by_columns,
             preferred_element_type=F32,
         )
 
-    product = product_of(slice(0, HALF), whole_one)
+    product = product_of(slice(0, FIRST), whole_one)
     wait_all(back_copy, 1, DP)
     for r in range(2):
-        rows = [back[i, :, r * SLICE : (r + 1) * SLICE] for i in range(DP)]
+        rows = [back[i, :, r * SLICE : (r + 1) * SLICE].astype(F32) for i in range(DP)]
         sums_out[16 * r : 16 * r + 16, :] = jnp.concatenate(rows, axis=1)[:, :width]
     total_squares = add_all(chip_copy, 0, tiles[2])
     factor = lax.rsqrt(total_squares / (R * FF) + norm_eps)[0:1, 0:1]
@@ -636,7 +640,7 @@
     pair_copy.wait_send()
     gather_one.drain()
     gather_two.end()
-    product += product_of(slice(HALF, R), whole_two)
+    product += product_of(slice(FIRST, R), whole_two)
     update[...] = (factor * product[:, :width]).astype(BF16)
     gather_two.drain()
 
@@ -654,8 +658,8 @@
             *PlaneSum.scratch(BF16),
             *PlaneSum.scratch(BF16),
             *PlaneSum.scratch(F32, PACKED // 2, LEAF),
-            *FoldedScatter.scratch(SLICE, HALF),
-            *FoldedScatter.scratch(SLICE, HALF),
+            *FoldedScatter.scratch(SLICE, FIRST),
+            *FoldedScatter.scratch(SLICE, R - FIRST),
             *FoldedGather.scratch(),
             *FoldedGather.scratch(),
             pltpu.VMEM((R, R), BF16),
@@ -664,20 +668,20 @@
             pltpu.VMEM((PACKED, LEAF), F32),
             pltpu.VMEM((R, R), BF16),
             pltpu.VMEM((WIDE, R), F32),
-            pltpu.VMEM((DP, 32, 2 * SLICE), F32),
-            pltpu.VMEM((DP, 32, 2 * SLICE), F32),
+            pltpu.VMEM((DP, 32, 2 * SLICE), BF16),
+            pltpu.VMEM((DP, 32, 2 * SLICE), BF16),
             pltpu.VMEM((DP, 16, R), BF16),
             pltpu.VMEM((DP - 1, 16, R), BF16),
             pltpu.VMEM((DP, 16, R), BF16),
             pltpu.VMEM((CHIPS, 2, 16, R), BF16),
             pltpu.VMEM((R, R), BF16),
             pltpu.VMEM((R, 2 * R), F32),
-            pltpu.VMEM((DP, 16, 2 * SLICE), F32),
-            pltpu.VMEM((DP, SLICE, HALF), BF16),
-            pltpu.VMEM((DP, SLICE, HALF), BF16),
-            pltpu.VMEM((DP, 16, 2 * SLICE), F32),
-            pltpu.VMEM((3, 8, 128), F32),
-            pltpu.VMEM((31, 8, 128), F32),
+            pltpu.VMEM((DP, 16, 2 * SLICE), BF16),
+            pltpu.VMEM((DP, SLICE, FIRST), BF16),
+            pltpu.VMEM((DP, SLICE, R - FIRST), BF16),
+            pltpu.VMEM((DP, 16, 2 * SLICE), BF16),
+            pltpu.VMEM((3, 1, 128), F32),
+            pltpu.VMEM((31, 1, 128), F32),
             *[sem for _ in range(7) for sem in dp_semaphores()],
             pltpu.SemaphoreType.DMA((2,)),
             pltpu.SemaphoreType.DMA((2,)),
@@ -689,10 +693,10 @@
             pltpu.SemaphoreType.DMA((5,)),
         ],
         compiler_params=pltpu.CompilerParams(
-            collective_id=0, has_side_effects=True, vmem_limit_bytes=60 * 2**20
+            collective_id=0, has_side_effects=True, vmem_limit_bytes=48 * 2**20
         ),
         name="galore_step",
-    )(out_grads.T, test_matrix, activations, first, second)
+    )(*(pltpu.with_memory_space_constraint(x, pltpu.HBM) for x in (out_grads.T, test_matrix, activations, first, second)))
 
 
 def shards(activations, out_grads, test_matrix, first_moment, second_moment):

time: 148 us -> 141 us (0.953)
  Pallas kernels: 143 us -> 139 us
    pallas_call x1, Pallas kernels: 143 us -> 139 us  [galore_call(): pl.pallas_call(galore_kernel, out_shape=(jax.ShapeDtypeStruct((R, first.s...]
where the time goes in v5:
time: 141 us
  Pallas kernels  139 us (99%)
    pallas_call x1, Pallas kernels, galore_call(): pl.pallas_call(galore_kernel, out_shape=(jax.ShapeDtypeStruct((R, first.s...  139 us

profile of v5, /device:TPU:1, one launch (start us, length us, event | category | flops | bytes accessed | tf_op | source)
XLA Modules:
  0.0 141.4 jit_solution(10093379995829687249)
XLA Ops:
  0.6 0.0 copy-start
  0.6 0.0 copy-start.1
  0.7 139.0 %galore_step.1 = (bf16[512,924]{1,0:T(8,128)(2,1)S(1)}, f32[32,924]{1,0:T(8,128)S(1)}) custom-call(bf16[924,512]{1,0:T(8,128)(2,1)} %bitcast.3, bf16[924,512]{1,0:T(8,128)(2,1)} %tm_in.1, bf16[512,256]{1,0:T(8,128)(2,1)} %act_in.1, f32[32,924]{1,0:T(8,128)} %first_in.1, f32[32,924]{1,0:T(8,128)} %second_in.1), custom_call_target="tpu_custom_call" | custom-call | tf_op jit(solution)/shard_map/galore_step/pallas_call | solution.py:649
  139.6 0.0 copy-done
  139.6 0.0 copy-done.1
  139.6 0.7 fusion
  140.4 1.0 copy.9
Async XLA Ops:
  0.6 139.0 %copy-start = (f32[32,924]{1,0:T(8,128)S(1)}, f32[32,924]{1,0:T(8,128)}, u32[]{:S(2)}) copy-start(f32[32,924]{1,0:T(8,128)} %first_in.1) | copy-start | bytes 354820
  0.6 139.0 %copy-start.1 = (f32[32,924]{1,0:T(8,128)S(1)}, f32[32,924]{1,0:T(8,128)}, u32[]{:S(2)}) copy-start(f32[32,924]{1,0:T(8,128)} %second_in.1) | copy-start | bytes 354820

commit v6 on v5

--- a/solution.py
+++ b/solution.py
@@ -65,6 +65,14 @@
     )
 
 
+def to_plane(copy_to):
+    def go(i, _):
+        copy_to(1 + (9 + i) % 15).start()
+        return 0
+
+    lax.fori_loop(0, CHIPS - 1, go, 0)
+
+
 def plane_scatter(stage, landed, sends, recvs):
     _, _, chip, core = place()
 
@@ -74,11 +82,7 @@
             stage.at[there], landed.at[k - 1], sends.at[k - 1], recvs.at[k - 1], {"mp": there * 2 + core}
         )
 
-    def go(k, _):
-        copy(k).start()
-        return 0
-
-    lax.fori_loop(1, CHIPS, go, 0)
+    to_plane(copy)
     return copy
 
 
@@ -89,11 +93,7 @@
         there = chip_at(chip, k)
         return send(block, block, sends.at[k - 1], recvs.at[k - 1], {"mp": there * 2 + core})
 
-    def go(k, _):
-        copy(k).start()
-        return 0
-
-    lax.fori_loop(1, CHIPS, go, 0)
+    to_plane(copy)
     return copy
 
 
@@ -613,11 +613,7 @@
     pair_copy.wait_recv()
     tiles[2] = tiles[1] + squares_in[0]
 
-    def chip_start(k, _):
-        chip_copy(k).start()
-        return 0
-
-    lax.fori_loop(1, CHIPS, chip_start, 0)
+    to_plane(chip_copy)
     gather_one.end()
 
     def product_of(columns, whole):

time: 141 us -> 141 us (level)
  no operation moved by 1% of the time
where the time goes in v6:
time: 141 us
  Pallas kernels  139 us (99%)
    pallas_call x1, Pallas kernels, galore_call(): pl.pallas_call(galore_kernel, out_shape=(jax.ShapeDtypeStruct((R, first.s...  139 us

profile of v6, /device:TPU:1, one launch (start us, length us, event | category | flops | bytes accessed | tf_op | source)
XLA Modules:
  0.0 141.2 jit_solution(6875743882711726952)
XLA Ops:
  0.6 0.0 copy-start
  0.6 0.0 copy-start.1
  0.7 138.8 %galore_step.1 = (bf16[512,924]{1,0:T(8,128)(2,1)S(1)}, f32[32,924]{1,0:T(8,128)S(1)}) custom-call(bf16[924,512]{1,0:T(8,128)(2,1)} %bitcast.3, bf16[924,512]{1,0:T(8,128)(2,1)} %tm_in.1, bf16[512,256]{1,0:T(8,128)(2,1)} %act_in.1, f32[32,924]{1,0:T(8,128)} %first_in.1, f32[32,924]{1,0:T(8,128)} %second_in.1), custom_call_target="tpu_custom_call" | custom-call | tf_op jit(solution)/shard_map/galore_step/pallas_call | solution.py:645
  139.5 0.0 copy-done
  139.5 0.0 copy-done.1
  139.5 0.7 fusion
  140.3 1.0 copy.9
Async XLA Ops:
  0.6 138.9 %copy-start = (f32[32,924]{1,0:T(8,128)S(1)}, f32[32,924]{1,0:T(8,128)}, u32[]{:S(2)}) copy-start(f32[32,924]{1,0:T(8,128)} %first_in.1) | copy-start | bytes 354820
  0.6 138.9 %copy-start.1 = (f32[32,924]{1,0:T(8,128)S(1)}, f32[32,924]{1,0:T(8,128)}, u32[]{:S(2)}) copy-start(f32[32,924]{1,0:T(8,128)} %second_in.1) | copy-start | bytes 354820
